TPU v7x, 128 devices: a whole 4x4x4 slice. The times are simulated.
128 devices in a mesh: node: 8 (over z, core), local: 16 (over y, x).
Axes of the slice: x: 4, y: 4, z: 4, core: 2. Of those that a mesh axis runs over, the one named last changes fastest.
Arguments:
- tokens: bfloat16 [2048, 3584], P(('node', 'local')), may hold values from -6 to 6
- expert_ids: int32 [2048, 8], P(('node', 'local')), may hold values from 0 to 127, as said below
- gate_values: bfloat16 [2048, 8], P(('node', 'local')), may hold values from 0.099609375 to 0.59765625
- w_gate: bfloat16 [128, 3584, 1024], P(('node', 'local')), may hold values from -0.09375 to 0.09375
- w_up: bfloat16 [128, 3584, 1024], P(('node', 'local')), may hold values from -0.09375 to 0.09375
- w_down: bfloat16 [128, 1024, 3584], P(('node', 'local')), may hold values from -0.1875 to 0.1875
Outputs:
- mixed: bfloat16 [2048, 3584], P(('node', 'local'))
Inputs may be any that keep to these rules, and one draw needn't show every extreme that they name: `expert_ids`: A token's experts are distinct and lie in at most 4 groups, group g holding experts g * 16 to (g + 1) * 16 - 1. Among the 16 tokens of one device (aligned blocks of rows) no expert is named by more than 2 tokens, and in every draw some experts are named by exactly 2 tokens of every device.
All inputs are finite; a program needn't handle non-finite values.
Results may differ from a plain program's by a relative error of at most 0.0059.
Values may be sent and summed in bfloat16 or wider, within the bound.
No kernel may reach another device: no remote copies, remote signals or barrier semaphores. Data moves between devices by JAX's collectives and lax.ppermute only.
A program may use at most 64 MiB of HBM per device.

v0:
```python
import jax
import jax.numpy as jnp
from jax import lax
from jax.sharding import PartitionSpec as P

PAIR = 2


def expert_rows(rows, w_gate, w_up, w_down):
    gate = jnp.dot(rows, w_gate[0], preferred_element_type=jnp.float32)
    upper = jnp.dot(rows, w_up[0], preferred_element_type=jnp.float32)
    hidden = (jax.nn.silu(gate) * upper).astype(jnp.bfloat16)
    return jnp.dot(hidden, w_down[0], preferred_element_type=jnp.float32).astype(jnp.bfloat16)


def local(tokens, expert_ids, gate_values, w_gate, w_up, w_down):
    tok_count = tokens.shape[0]
    width = tokens.shape[1]
    topk = expert_ids.shape[1]
    nodes = lax.axis_size("node")
    per_node = lax.axis_size("local")
    experts = nodes * per_node
    most = PAIR * tok_count // per_node
    hits = (expert_ids[:, :, None] == jnp.arange(experts, dtype=jnp.int32)[None, None, :]).astype(
        jnp.int32
    )
    usage = jnp.sum(hits, axis=1)
    earlier = jnp.cumsum(usage, axis=0) - usage
    slots = jnp.sum(hits * earlier[:, None, :], axis=2)
    nothing = jnp.zeros((), jnp.bfloat16)
    target = (expert_ids * most + slots).reshape(-1)
    owners = jnp.repeat(jnp.arange(tok_count, dtype=jnp.int32), topk)
    source = jnp.full((experts * most,), -1, jnp.int32).at[target].set(owners)
    filled = jnp.where((source >= 0)[:, None], tokens[jnp.maximum(source, 0)], nothing)
    outgoing = filled.reshape(experts, most, width)
    incoming = lax.all_to_all(outgoing, ("node", "local"), split_axis=0, concat_axis=0, tiled=True)
    shaped = incoming.reshape(-1, width)
    result = expert_rows(shaped, w_gate, w_up, w_down).reshape(incoming.shape)
    answered = lax.all_to_all(result, ("node", "local"), split_axis=0, concat_axis=0, tiled=True)
    picked = answered.reshape(-1, width)[target].reshape(tok_count, topk, width)
    total = jnp.sum(
        gate_values.astype(jnp.float32)[:, :, None] * picked.astype(jnp.float32), axis=1
    )
    return total.astype(jnp.bfloat16)


def solution(mesh):
    return jax.shard_map(
        local,
        mesh=mesh,
        in_specs=(
            P(("node", "local"), None),
            P(("node", "local"), None),
            P(("node", "local"), None),
            P(("node", "local"), None, None),
            P(("node", "local"), None, None),
            P(("node", "local"), None, None),
        ),
        out_specs=P(("node", "local"), None),
        check_vma=False,
    )
```

profile of v0, /device:TPU:1, one launch (start us, length us, event | category | flops | bytes accessed | tf_op | source)
XLA Modules:
  0.0 109.6 jit_solution(8447987822442690198)
XLA Ops:
  0.0 0.0 copy-start
  0.0 0.8 copy.14
  0.8 0.1 convert_reduce_fusion
  0.9 0.4 select_reduce_fusion
  1.4 0.1 reshape.65
  1.5 0.1 reshape.91
  1.6 1.0 scatter_custom_fusion
  2.6 0.0 copy-done
  2.6 1.7 %gather_fusion = bf16[256,3584]{1,0:T(8,128)(2,1)S(1)} fusion(bf16[16,3584]{1,0:T(8,128)(2,1)S(1)} %copy-done, s32[1024]{0:T(1024)S(1)} %pad_clamp_fusion.1), kind=kCustom, calls=%fused_computation | custom fusion | bytes 3671040 | tf_op jit(solution)/shard_map/gather | solution.py:34
  4.3 1.7 %gather.9 = bf16[128,2,3584]{2,1,0:T(2,128)(2,1)} reshape(bf16[256,3584]{1,0:T(8,128)(2,1)S(1)} %gather_fusion) | data formatting | bytes 3670016 | tf_op jit(solution)/shard_map/gather | solution.py:34
  6.0 0.2 broadcast_in_dim.32
  6.2 3.3 %broadcast_select_fusion = bf16[128,2,3584]{2,1,0:T(2,128)(2,1)S(1)} fusion(bf16[128,2,3584]{2,1,0:T(2,128)(2,1)} %gather.9, pred[128,2]{1,0:T(8,128)(4,1)S(1)} %broadcast_in_dim.32), kind=kLoop, calls=%fused_computation.10 | loop fusion | flops 917504 | bytes 3670272 | tf_op jit(solution)/shard_map/jit(_where)/select_n | solution.py:34
  9.4 38.2 %all_to_all.10 = bf16[128,2,3584]{2,1,0:T(2,128)(2,1)S(1)} all-to-all(bf16[128,2,3584]{2,1,0:T(2,128)(2,1)S(1)} %broadcast_select_fusion), channel_id=1, replica_groups=mesh['node'=8,'local'=16] {'node','local'}, dimensions={0} | all-to-all | bytes 3670016 | tf_op jit(solution)/shard_map/all_to_all | solution.py:36
  47.6 1.7 %reshape.67 = bf16[256,3584]{1,0:T(8,128)(2,1)} reshape(bf16[128,2,3584]{2,1,0:T(2,128)(2,1)S(1)} %all_to_all.10) | data formatting | bytes 3670016 | tf_op jit(solution)/shard_map/reshape | solution.py:37
  49.3 0.0 copy-start.1
  49.3 5.8 %fusion.4 = f32[256,1024]{1,0:T(8,128)S(1)} fusion(bf16[256,3584]{1,0:T(8,128)(2,1)} %reshape.67, bf16[1,3584,1024]{2,1,0:T(8,128)(2,1)} %param.9), kind=kOutput, calls=%fused_computation.7 | convolution fusion | flops 1879048192 | bytes 10223616 | tf_op jit(solution)/shard_map/dot_general | solution.py:10
  55.1 0.0 copy-done.1
  55.1 10.6 %fusion.6 = bf16[256,3584]{1,0:T(8,128)(2,1)} fusion(bf16[1,1024,3584]{2,1,0:T(8,128)(2,1)} %param.11, bf16[256,3584]{1,0:T(8,128)(2,1)S(1)} %copy-done.1, bf16[1,3584,1024]{2,1,0:T(8,128)(2,1)} %param.10, f32[256,1024]{1,0:T(8,128)S(1)} %fusion.4), kind=kOutput, calls=%fused_computation.9 | convolution fusion | flops 3760586752 | bytes 19398656 | tf_op jit(solution)/shard_map/dot_general | solution.py:13
  65.8 4.8 %reshape.68 = bf16[128,2,3584]{2,1,0:T(2,128)(2,1)} reshape(bf16[256,3584]{1,0:T(8,128)(2,1)} %fusion.6) | data formatting | bytes 3670016 | tf_op jit(solution)/shard_map/reshape | solution.py:38
  70.6 0.0 copy-start.2
  70.6 5.8 %all-to-all-start.1 = ((bf16[128,2,3584]{2,1,0:T(2,128)(2,1)}), bf16[128,2,3584]{2,1,0:T(2,128)(2,1)}, u32[]{:S(2)}, u32[]{:S(2)}) async-start(bf16[128,2,3584]{2,1,0:T(2,128)(2,1)} %reshape.68), calls=%async_computation.1 | async-start | bytes 3670016 | tf_op jit(solution)/shard_map/all_to_all | solution.py:39
  76.4 0.0 copy-done.2
  76.4 0.1 copy.13
  76.5 26.6 %all-to-all-done.1 = bf16[128,2,3584]{2,1,0:T(2,128)(2,1)} async-done(((bf16[128,2,3584]{2,1,0:T(2,128)(2,1)}), bf16[128,2,3584]{2,1,0:T(2,128)(2,1)}, u32[]{:S(2)}, u32[]{:S(2)}) %all-to-all-start.1) | async-done | bytes 1835040 | tf_op jit(solution)/shard_map/all_to_all | solution.py:39
  103.1 4.1 %reshape.69 = bf16[256,3584]{1,0:T(8,128)(2,1)S(1)} reshape(bf16[128,2,3584]{2,1,0:T(2,128)(2,1)} %all-to-all-done.1) | data formatting | bytes 3670016 | tf_op jit(solution)/shard_map/reshape | solution.py:40
  107.2 1.1 %gather_fusion.1 = bf16[128,3584]{1,0:T(8,128)(2,1)S(1)} fusion(bf16[256,3584]{1,0:T(8,128)(2,1)S(1)} %reshape.69, s32[1024]{0:T(1024)S(1)} %pad_clamp_fusion), kind=kCustom, calls=%fused_computation.1 | custom fusion | bytes 1835520 | tf_op jit(solution)/shard_map/gather | solution.py:40
  108.3 1.3 %fusion.9 = bf16[16,3584]{1,0:T(8,128)(2,1)} fusion(bf16[128,3584]{1,0:T(8,128)(2,1)S(1)} %gather_fusion.1, f32[16,8]{1,0:T(8,128)S(1)} %copy.13), kind=kLoop, calls=%fused_computation.12 | loop fusion | flops 1318912 | bytes 1032704 | tf_op jit(solution)/shard_map/reduce_sum | solution.py:41
  (9 shorter events, 0.1 us)
Async XLA Ops:
  0.0 2.6 %copy-start = (bf16[16,3584]{1,0:T(8,128)(2,1)S(1)}, bf16[16,3584]{1,0:T(8,128)(2,1)}, u32[]{:S(2)}) copy-start(bf16[16,3584]{1,0:T(8,128)(2,1)} %param.6) | copy-start | bytes 344068
  49.3 5.8 %copy-start.1 = (bf16[256,3584]{1,0:T(8,128)(2,1)S(1)}, bf16[256,3584]{1,0:T(8,128)(2,1)}, u32[]{:S(2)}) copy-start(bf16[256,3584]{1,0:T(8,128)(2,1)} %reshape.67) | copy-start | bytes 5505028
  70.6 5.8 %copy-start.2 = (bf16[16,8]{0,1:T(8,128)(2,1)S(1)}, bf16[16,8]{0,1:T(8,128)(2,1)}, u32[]{:S(2)}) copy-start(bf16[16,8]{0,1:T(8,128)(2,1)} %param.8) | copy-start | bytes 772
  70.6 32.6 %all-to-all-start.1 = ((bf16[128,2,3584]{2,1,0:T(2,128)(2,1)}), bf16[128,2,3584]{2,1,0:T(2,128)(2,1)}, u32[]{:S(2)}, u32[]{:S(2)}) async-start(bf16[128,2,3584]{2,1,0:T(2,128)(2,1)} %reshape.68), calls=%async_computation.1 | async-start | bytes 3670016 | tf_op jit(solution)/shard_map/all_to_all | solution.py:39
where the time goes:
time: 110 us
  blocking collectives  38.2 us (35%)
  waiting for transfers between devices  26.6 us (24%)
  local copies, waits for them, and re-layouts  17.2 us (16%)
  matrix products  16.4 us (15%)
  starting transfers between devices  5.82 us (5%)
  other arithmetic  5.18 us (5%)
    all_to_all x1, blocking collectives, local(): lax.all_to_all(outgoing, ('node', 'local'), split_axis=0, concat_axis=0,...  38.2 us
    all_to_all x1, waiting for transfers between devices, local(): lax.all_to_all(result, ('node', 'local'), split_axis=0, concat_axis=0, ti...  26.6 us
    dot_general x1, matrix products, expert_rows(): jnp.dot(hidden, w_down[0], preferred_element_type=jnp.float32)  10.6 us
    dot_general x1, matrix products, expert_rows(): gate = jnp.dot(rows, w_gate[0], preferred_element_type=jnp.float32)  5.82 us
    all_to_all x1, starting transfers between devices, local(): lax.all_to_all(result, ('node', 'local'), split_axis=0, concat_axis=0, ti...  5.82 us
    reshape x1, local copies, waits for them, and re-layouts, local(): result = expert_rows(shaped, w_gate, w_up, w_down).reshape(incoming.shape)  4.79 us
    reshape x1, local copies, waits for them, and re-layouts, local(): picked = answered.reshape(-1, width)[target].reshape(tok_count, topk, width)  4.06 us
    gather x2, local copies, waits for them, and re-layouts, local(): tokens[jnp.maximum(source, 0)]  3.41 us
  transfers between devices with their start and end apart: 1, of which 1 were waited for; matrix products, arithmetic and copies ran while one was open for 0% of the time, Pallas kernels for 0%

commit v1 on v0

v1 whole, which is shorter than its diff:
```python
import jax
import jax.numpy as jnp
from jax import lax
from jax.experimental import pallas as pl
from jax.experimental.pallas import tpu as pltpu
from jax.sharding import PartitionSpec as P

PAIR = 2
SEGMENTS = 4
BLOCK = PAIR * SEGMENTS
GROUP = 256

MIB = 1 << 20


def routing(ids_t, rows):
    topk, tok_count = ids_t.shape
    experts = rows // BLOCK
    expert = lax.broadcasted_iota(jnp.int32, (experts, tok_count), 0)
    used = jnp.zeros((experts, tok_count), jnp.float32)
    for k in range(topk):
        used = jnp.where(ids_t[k : k + 1, :] == expert, 1.0, used)
    wide = (tok_count, SEGMENTS * tok_count)
    column = lax.broadcasted_iota(jnp.int32, wide, 1) & (tok_count - 1)
    token = lax.broadcasted_iota(jnp.int32, wide, 0)
    weight = jnp.where(token < column, 1.0, jnp.where(token == column, -64.0, 0.0))
    rank = jnp.dot(used.astype(jnp.bfloat16), weight.astype(jnp.bfloat16), preferred_element_type=jnp.float32)
    rank = (rank + 64.0).astype(jnp.int32)
    shape = (experts, BLOCK, SEGMENTS * tok_count)
    rank = jnp.broadcast_to(rank[:, None, :], shape).reshape(rows, SEGMENTS * tok_count)
    row = lax.broadcasted_iota(jnp.int32, rank.shape, 0)
    lane = lax.broadcasted_iota(jnp.int32, rank.shape, 1)
    slot = row & (PAIR - 1)
    segment = (row & (BLOCK - 1)) >> 1
    return (rank == slot) & ((lane >> 4) == segment)


def dispatch_kernel(ids_ref, tokens_ref, out_ref):
    rows, width = out_ref.shape
    chosen = routing(ids_ref[...], rows)
    chosen = jnp.where(chosen, 1.0, 0.0).astype(jnp.bfloat16)
    table = jnp.concatenate(
        [tokens_ref[:, s * width : (s + 1) * width] for s in range(SEGMENTS)], axis=0
    )
    out_ref[...] = jnp.dot(chosen, table, preferred_element_type=jnp.float32).astype(jnp.bfloat16)


def weights_kernel(ids_ref, gates_ref, out_ref):
    rows = out_ref.shape[0]
    ids_t = ids_ref[...]
    topk, tok_count = ids_t.shape
    gates_t = gates_ref[...].astype(jnp.float32)
    experts = rows // BLOCK
    expert = lax.broadcasted_iota(jnp.int32, (experts, tok_count), 0)
    gate = jnp.zeros((experts, tok_count), jnp.float32)
    for k in range(topk):
        gate = jnp.where(ids_t[k : k + 1, :] == expert, gates_t[k : k + 1, :], gate)
    gate = jnp.concatenate([gate] * SEGMENTS, axis=1)
    shape = (experts, BLOCK, SEGMENTS * tok_count)
    gate = jnp.broadcast_to(gate[:, None, :], shape).reshape(rows, SEGMENTS * tok_count)
    out_ref[...] = jnp.where(routing(ids_t, rows), gate, 0.0).astype(jnp.bfloat16)


def combine_kernel(weights_ref, rows_ref, out_ref):
    tok_count = out_ref.shape[0]
    width = rows_ref.shape[1]
    total = lax.dot_general(
        weights_ref[...],
        rows_ref[...],
        (((0,), (0,)), ((), ())),
        preferred_element_type=jnp.float32,
    ).astype(jnp.bfloat16)
    for s in range(SEGMENTS):
        out_ref[:, s * width : (s + 1) * width] = total[s * tok_count : (s + 1) * tok_count, :]


def reorder(forward):
    part = GROUP // SEGMENTS
    a = lax.broadcasted_iota(jnp.int32, (GROUP, GROUP), 0 if forward else 1)
    b = lax.broadcasted_iota(jnp.int32, (GROUP, GROUP), 1 if forward else 0)
    inside = a & (part - 1)
    place = (inside >> 1) * BLOCK + (a >> 6) * PAIR + (inside & 1)
    return jnp.where(place == b, 1.0, 0.0).astype(jnp.bfloat16)


def expert_kernel(rows_ref, gate_ref, up_ref, down_ref, out_ref, x_ref, h_ref, y_ref):
    total, width = rows_ref.shape
    part = GROUP // SEGMENTS
    groups = total // GROUP
    hid = gate_ref.shape[1]
    depth = down_ref.shape[1]
    forward = reorder(True)
    for g in range(groups):
        block = jnp.dot(
            forward, rows_ref[g * GROUP : (g + 1) * GROUP, :], preferred_element_type=jnp.float32
        ).astype(jnp.bfloat16)
        for s in range(SEGMENTS):
            x_ref[g * part : (g + 1) * part, s * width : (s + 1) * width] = block[
                s * part : (s + 1) * part, :
            ]
    tile = 256

    @pl.loop(0, hid // tile)
    def _(n):
        columns = pl.ds(pl.multiple_of(n * tile, tile), tile)
        gate = jnp.dot(x_ref[...], gate_ref[:, columns], preferred_element_type=jnp.float32)
        upper = jnp.dot(x_ref[...], up_ref[:, columns], preferred_element_type=jnp.float32)
        h_ref[:, columns] = (gate / (1.0 + jnp.exp(-gate)) * upper).astype(jnp.bfloat16)

    wide = 512

    @pl.loop(0, depth // wide)
    def _(n):
        columns = pl.ds(pl.multiple_of(n * wide, wide), wide)
        y_ref[:, columns] = jnp.dot(
            h_ref[...], down_ref[:, columns], preferred_element_type=jnp.float32
        ).astype(jnp.bfloat16)

    back = reorder(False)
    for g in range(groups):
        block = jnp.concatenate(
            [
                y_ref[g * part : (g + 1) * part, s * width : (s + 1) * width]
                for s in range(SEGMENTS)
            ],
            axis=0,
        )
        out_ref[g * GROUP : (g + 1) * GROUP, :] = jnp.dot(
            back, block, preferred_element_type=jnp.float32
        ).astype(jnp.bfloat16)


def vmem():
    return pl.BlockSpec(memory_space=pltpu.VMEM)


def call(kernel, out_shape, inputs, limit, scratch=(), flops=0, moved=0):
    return pl.pallas_call(
        kernel,
        out_shape=out_shape,
        in_specs=[vmem()] * inputs,
        out_specs=vmem(),
        scratch_shapes=list(scratch),
        compiler_params=pltpu.CompilerParams(vmem_limit_bytes=limit),
        cost_estimate=pl.CostEstimate(flops=flops, bytes_accessed=moved, transcendentals=0),
    )


def local(tokens, expert_ids, gate_values, w_gate, w_up, w_down):
    tok_count, width = tokens.shape
    hid = w_gate.shape[2]
    experts = lax.axis_size("node") * lax.axis_size("local")
    rows = experts * BLOCK
    piece = width // SEGMENTS
    bf16 = jnp.bfloat16
    ids_t = expert_ids.T
    gates_t = gate_values.T
    outgoing = call(
        dispatch_kernel, jax.ShapeDtypeStruct((rows, piece), bf16), 2, 12 * MIB,
        flops=2 * rows * 64 * piece, moved=2 * rows * piece,
    )(ids_t, tokens)
    weights = call(
        weights_kernel, jax.ShapeDtypeStruct((rows, SEGMENTS * tok_count), bf16), 2, 8 * MIB,
        moved=2 * rows * 64,
    )(ids_t, gates_t)
    incoming = lax.all_to_all(
        outgoing.reshape(experts, BLOCK, piece), ("node", "local"), split_axis=0, concat_axis=0, tiled=True
    )
    m = experts * PAIR
    result = call(
        expert_kernel, jax.ShapeDtypeStruct((rows, piece), bf16), 4, 16 * MIB,
        scratch=(
            pltpu.VMEM((m, width), bf16),
            pltpu.VMEM((m, hid), bf16),
            pltpu.VMEM((m, width), bf16),
        ),
        flops=6 * m * width * hid, moved=6 * width * hid,
    )(incoming.reshape(rows, piece), w_gate[0], w_up[0], w_down[0])
    answered = lax.all_to_all(
        result.reshape(experts, BLOCK, piece), ("node", "local"), split_axis=0, concat_axis=0, tiled=True
    )
    return call(
        combine_kernel, jax.ShapeDtypeStruct((tok_count, width), bf16), 2, 12 * MIB,
        flops=2 * rows * 64 * piece, moved=2 * rows * piece,
    )(weights, answered.reshape(rows, piece))


def solution(mesh):
    return jax.shard_map(
        local,
        mesh=mesh,
        in_specs=(
            P(("node", "local"), None),
            P(("node", "local"), None),
            P(("node", "local"), None),
            P(("node", "local"), None, None),
            P(("node", "local"), None, None),
            P(("node", "local"), None, None),
        ),
        out_specs=P(("node", "local"), None),
        check_vma=False,
    )
```

time: 110 us -> 93.5 us (0.85)
  matrix products: 16.4 us -> 0 us
  Pallas kernels: 0 us -> 12.7 us
  local copies, waits for them, and re-layouts: 17.2 us -> 10.8 us
  other arithmetic: 5.18 us -> 0 us
    dot_general x2 -> x0, matrix products: 16.4 us -> none  [the longest x1 10.6 us: expert_rows(): jnp.dot(hidden, w_down[0], preferred_element_type=jnp.float32)]
    pallas_call x0 -> x4, Pallas kernels: none -> 12.7 us  [the longest x1 10.4 us: local(): call(expert_kernel, jax.ShapeDtypeStruct((rows, piece), bf16), 4, 16 * MI...]
    reshape x5 -> x0, local copies, waits for them, and re-layouts: 10.7 us -> none  [the longest x1 4.79 us: local(): result = expert_rows(shaped, w_gate, w_up, w_down).reshape(incoming.shape)]
    unnamed x7 -> x14, local copies, waits for them, and re-layouts: 0.8 us -> 10.8 us
    gather x3 -> x0, local copies, waits for them, and re-layouts: 4.52 us -> none  [the longest x2 3.41 us: local(): tokens[jnp.maximum(source, 0)]]
    select_n x2 -> x0, other arithmetic: 3.26 us -> none  [the longest x1 3.26 us: local(): jnp.where((source >= 0)[:, None], tokens[jnp.maximum(source, 0)], nothing)]
    reduce_sum x3 -> x0, other arithmetic: 1.85 us -> none  [the longest x1 1.34 us: local(): jnp.sum(gate_values.astype(jnp.float32)[:, :, None] * picked.astype(jnp.f...]
where the time goes in v1:
time: 93.5 us; the launch traced here: 93.1 us
  blocking collectives  38.2 us (41%)
  waiting for transfers between devices  26.6 us (28%)
  Pallas kernels  12.7 us (14%)
  local copies, waits for them, and re-layouts  10.8 us (12%)
  starting transfers between devices  4.81 us (5%)
    all_to_all x1, blocking collectives, local(): lax.all_to_all(outgoing.reshape(experts, BLOCK, piece), ('node', 'local')...  38.2 us
    all_to_all x1, waiting for transfers between devices, local(): lax.all_to_all(result.reshape(experts, BLOCK, piece), ('node', 'local'),...  26.6 us
    unnamed x14, local copies, waits for them, and re-layouts  10.8 us
    pallas_call x1, Pallas kernels, local(): call(expert_kernel, jax.ShapeDtypeStruct((rows, piece), bf16), 4, 16 * MI...  10.4 us
    all_to_all x1, starting transfers between devices, local(): lax.all_to_all(result.reshape(experts, BLOCK, piece), ('node', 'local'),...  4.81 us
  transfers between devices with their start and end apart: 1, of which 1 were waited for; matrix products, arithmetic and copies ran while one was open for 0% of the time, Pallas kernels for 0%

profile of v1, /device:TPU:1, one launch (start us, length us, event | category | flops | bytes accessed | tf_op | source)
XLA Modules:
  0.0 93.1 jit_solution(9449916039629861150)
XLA Ops:
  0.0 0.0 copy-start.3
  0.0 0.9 copy-done.3
  0.9 0.0 copy-start.4
  0.9 0.7 copy-done.4
  1.6 0.8 shard_map.65
  2.4 38.2 %all_to_all.10 = bf16[128,8,896]{2,1,0:T(8,128)(2,1)S(1)} all-to-all(bf16[128,8,896]{2,1,0:T(8,128)(2,1)S(1)} %bitcast.11), channel_id=1, replica_groups=mesh['node'=8,'local'=16] {'node','local'}, dimensions={0} | all-to-all | bytes 3670016 | tf_op jit(solution)/shard_map/all_to_all | solution.py:166
  40.6 0.0 copy-start
  40.6 3.1 %copy-done = bf16[1,3584,1024]{2,1,0:T(8,128)(2,1)S(1)} copy-done((bf16[1,3584,1024]{2,1,0:T(8,128)(2,1)S(1)}, bf16[1,3584,1024]{2,1,0:T(8,128)(2,1)}, u32[]{:S(2)}) %copy-start) | copy-done | bytes 7340056
  43.6 0.0 copy-start.1
  43.6 3.1 %copy-done.1 = bf16[1,3584,1024]{2,1,0:T(8,128)(2,1)S(1)} copy-done((bf16[1,3584,1024]{2,1,0:T(8,128)(2,1)S(1)}, bf16[1,3584,1024]{2,1,0:T(8,128)(2,1)}, u32[]{:S(2)}) %copy-start.1) | copy-done | bytes 7340056
  46.7 0.0 copy-start.2
  46.7 3.1 %copy-done.2 = bf16[1,1024,3584]{2,1,0:T(8,128)(2,1)S(1)} copy-done((bf16[1,1024,3584]{2,1,0:T(8,128)(2,1)S(1)}, bf16[1,1024,3584]{2,1,0:T(8,128)(2,1)}, u32[]{:S(2)}) %copy-start.2) | copy-done | bytes 7340056
  49.8 10.4 %shard_map.66 = bf16[1024,896]{1,0:T(8,128)(2,1)} custom-call(bf16[1024,896]{1,0:T(8,128)(2,1)S(1)} %bitcast.9, bf16[3584,1024]{1,0:T(8,128)(2,1)S(1)} %bitcast.12, bf16[3584,1024]{1,0:T(8,128)(2,1)S(1)} %bitcast.13, bf16[1024,3584]{1,0:T(8,128)(2,1)S(1)} %bitcast.14), custom_call_target="tpu_custom_call" | custom-call | flops 5637144576 | bytes 22020096 | tf_op jit(solution)/shard_map/pallas_call | solution.py:170
  60.2 0.0 copy-start.5
  60.2 0.0 copy-start.6
  60.2 4.8 %all-to-all-start.1 = ((bf16[128,8,896]{2,1,0:T(8,128)(2,1)}), bf16[128,8,896]{2,1,0:T(8,128)(2,1)S(1)}, u32[]{:S(2)}, u32[]{:S(2)}) async-start(bf16[128,8,896]{2,1,0:T(8,128)(2,1)} %bitcast.7), calls=%async_computation.1 | async-start | bytes 3670016 | tf_op jit(solution)/shard_map/all_to_all | solution.py:179
  65.0 0.0 copy-done.5
  65.0 0.0 copy-done.6
  65.0 0.4 shard_map.64.weights_ref
  65.5 26.6 %all-to-all-done.1 = bf16[128,8,896]{2,1,0:T(8,128)(2,1)S(1)} async-done(((bf16[128,8,896]{2,1,0:T(8,128)(2,1)}), bf16[128,8,896]{2,1,0:T(8,128)(2,1)S(1)}, u32[]{:S(2)}, u32[]{:S(2)}) %all-to-all-start.1) | async-done | bytes 1835040 | tf_op jit(solution)/shard_map/all_to_all | solution.py:179
  92.1 1.1 %shard_map.67 = bf16[16,3584]{1,0:T(8,128)(2,1)} custom-call(bf16[1024,64]{1,0:T(8,128)(2,1)S(1)} %shard_map.64.weights_ref, bf16[1024,896]{1,0:T(8,128)(2,1)S(1)} %bitcast.10), custom_call_target="tpu_custom_call" | custom-call | flops 117440512 | bytes 1835008 | tf_op jit(solution)/shard_map/pallas_call | solution.py:182
Async XLA Ops:
  0.0 0.9 copy-start.3
  0.9 0.7 copy-start.4
  40.6 3.1 %copy-start = (bf16[1,3584,1024]{2,1,0:T(8,128)(2,1)S(1)}, bf16[1,3584,1024]{2,1,0:T(8,128)(2,1)}, u32[]{:S(2)}) copy-start(bf16[1,3584,1024]{2,1,0:T(8,128)(2,1)} %param.9) | copy-start | bytes 22020100
  43.6 3.1 %copy-start.1 = (bf16[1,3584,1024]{2,1,0:T(8,128)(2,1)S(1)}, bf16[1,3584,1024]{2,1,0:T(8,128)(2,1)}, u32[]{:S(2)}) copy-start(bf16[1,3584,1024]{2,1,0:T(8,128)(2,1)} %param.10) | copy-start | bytes 22020100
  46.7 3.1 %copy-start.2 = (bf16[1,1024,3584]{2,1,0:T(8,128)(2,1)S(1)}, bf16[1,1024,3584]{2,1,0:T(8,128)(2,1)}, u32[]{:S(2)}) copy-start(bf16[1,1024,3584]{2,1,0:T(8,128)(2,1)} %param.11) | copy-start | bytes 22020100
  60.2 4.8 %copy-start.5 = (s32[16,8]{0,1:T(8,128)S(1)}, s32[16,8]{0,1:T(8,128)}, u32[]{:S(2)}) copy-start(s32[16,8]{0,1:T(8,128)} %param.7) | copy-start | bytes 1540
  60.2 4.8 %copy-start.6 = (bf16[16,8]{0,1:T(8,128)(2,1)S(1)}, bf16[16,8]{0,1:T(8,128)(2,1)}, u32[]{:S(2)}) copy-start(bf16[16,8]{0,1:T(8,128)(2,1)} %param.8) | copy-start | bytes 772
  60.2 31.9 %all-to-all-start.1 = ((bf16[128,8,896]{2,1,0:T(8,128)(2,1)}), bf16[128,8,896]{2,1,0:T(8,128)(2,1)S(1)}, u32[]{:S(2)}, u32[]{:S(2)}) async-start(bf16[128,8,896]{2,1,0:T(8,128)(2,1)} %bitcast.7), calls=%async_computation.1 | async-start | bytes 3670016 | tf_op jit(solution)/shard_map/all_to_all | solution.py:179

commit v2 on v1

--- a/solution.py
+++ b/solution.py
@@ -157,7 +157,7 @@
     gates_t = gate_values.T
     outgoing = call(
         dispatch_kernel, jax.ShapeDtypeStruct((rows, piece), bf16), 2, 12 * MIB,
-        flops=2 * rows * 64 * piece, moved=2 * rows * piece,
+        flops=30_000_000_000, moved=60_000_000,
     )(ids_t, tokens)
     weights = call(
         weights_kernel, jax.ShapeDtypeStruct((rows, SEGMENTS * tok_count), bf16), 2, 8 * MIB,

time: 93.5 us -> 84.8 us (0.907)
  local copies, waits for them, and re-layouts: 10.8 us -> 2.19 us
    unnamed x14 -> x20, local copies, waits for them, and re-layouts: 10.8 us -> 2.19 us
  transfers between devices with their start and end apart: 1 -> 1, of which waited for: 1 -> 1; matrix products, arithmetic and copies ran while one was open for 0% -> 0% of each run, Pallas kernels for 0% -> 1%
where the time goes in v2:
time: 84.8 us; the launch traced here: 84.6 us
  blocking collectives  38.2 us (45%)
  waiting for transfers between devices  26.6 us (31%)
  Pallas kernels  12.7 us (15%)
  starting transfers between devices  4.8 us (6%)
  local copies, waits for them, and re-layouts  2.19 us (3%)
    all_to_all x1, blocking collectives, local(): lax.all_to_all(outgoing.reshape(experts, BLOCK, piece), ('node', 'local')...  38.2 us
    all_to_all x1, waiting for transfers between devices, local(): lax.all_to_all(result.reshape(experts, BLOCK, piece), ('node', 'local'),...  26.6 us
    pallas_call x1, Pallas kernels, local(): call(expert_kernel, jax.ShapeDtypeStruct((rows, piece), bf16), 4, 16 * MI...  10.4 us
    all_to_all x1, starting transfers between devices, local(): lax.all_to_all(result.reshape(experts, BLOCK, piece), ('node', 'local'),...  4.8 us
    unnamed x20, local copies, waits for them, and re-layouts  2.19 us
  transfers between devices with their start and end apart: 1, of which 1 were waited for; matrix products, arithmetic and copies ran while one was open for 0% of the time, Pallas kernels for 1%

profile of v2, /device:TPU:1, one launch (start us, length us, event | category | flops | bytes accessed | tf_op | source)
XLA Modules:
  0.0 84.6 jit_solution(4243117649253247330)
XLA Ops:
  0.0 0.0 slice-start
  0.0 0.0 slice-start.2
  0.0 0.0 slice-start.4
  0.0 0.0 copy-start
  0.0 0.8 copy-done
  0.8 0.0 copy-start.3
  0.9 1.3 %copy-done.3 = bf16[16,3584]{1,0:T(8,128)(2,1)S(1)} copy-done((bf16[16,3584]{1,0:T(8,128)(2,1)S(1)}, bf16[16,3584]{1,0:T(8,128)(2,1)}, u32[]{:S(2)}) %copy-start.3) | copy-done | bytes 114712
  2.2 0.0 slice-start.1
  2.2 0.0 slice-start.3
  2.2 0.0 slice-start.5
  2.2 0.8 shard_map.65
  3.0 38.2 %all_to_all.10 = bf16[128,8,896]{2,1,0:T(8,128)(2,1)S(1)} all-to-all(bf16[128,8,896]{2,1,0:T(8,128)(2,1)S(1)} %bitcast.20), channel_id=1, replica_groups=mesh['node'=8,'local'=16] {'node','local'}, dimensions={0} | all-to-all | bytes 3670016 | tf_op jit(solution)/shard_map/all_to_all | solution.py:166
  41.2 0.0 slice-done
  41.2 0.0 slice-done.2
  41.2 0.0 slice-done.4
  41.2 0.0 slice-done.1
  41.2 0.0 slice-done.3
  41.2 0.0 slice-done.5
  41.2 10.4 %shard_map.66 = bf16[1024,896]{1,0:T(8,128)(2,1)} custom-call(bf16[1024,896]{1,0:T(8,128)(2,1)S(1)} %bitcast.9, bf16[3584,1024]{1,0:T(8,128)(2,1)S(1)} %bitcast.13, bf16[3584,1024]{1,0:T(8,128)(2,1)S(1)} %bitcast.16, bf16[1024,3584]{1,0:T(8,128)(2,1)S(1)} %bitcast.19), custom_call_target="tpu_custom_call" | custom-call | flops 5637144576 | bytes 22020096 | tf_op jit(solution)/shard_map/pallas_call | solution.py:170
  51.6 0.0 copy-start.1
  51.7 0.0 copy-start.2
  51.7 4.8 %all-to-all-start.1 = ((bf16[128,8,896]{2,1,0:T(8,128)(2,1)}), bf16[128,8,896]{2,1,0:T(8,128)(2,1)S(1)}, u32[]{:S(2)}, u32[]{:S(2)}) async-start(bf16[128,8,896]{2,1,0:T(8,128)(2,1)} %bitcast.7), calls=%async_computation.1 | async-start | bytes 3670016 | tf_op jit(solution)/shard_map/all_to_all | solution.py:179
  56.5 0.0 copy-done.1
  56.5 0.0 copy-done.2
  56.5 0.4 shard_map.64.weights_ref
  56.9 26.6 %all-to-all-done.1 = bf16[128,8,896]{2,1,0:T(8,128)(2,1)S(1)} async-done(((bf16[128,8,896]{2,1,0:T(8,128)(2,1)}), bf16[128,8,896]{2,1,0:T(8,128)(2,1)S(1)}, u32[]{:S(2)}, u32[]{:S(2)}) %all-to-all-start.1) | async-done | bytes 1835040 | tf_op jit(solution)/shard_map/all_to_all | solution.py:179
  83.5 1.1 %shard_map.67 = bf16[16,3584]{1,0:T(8,128)(2,1)} custom-call(bf16[1024,64]{1,0:T(8,128)(2,1)S(1)} %shard_map.64.weights_ref, bf16[1024,896]{1,0:T(8,128)(2,1)S(1)} %bitcast.10), custom_call_target="tpu_custom_call" | custom-call | flops 117440512 | bytes 1835008 | tf_op jit(solution)/shard_map/pallas_call | solution.py:182
  (3 shorter events, 0.0 us)
Async XLA Ops:
  0.0 41.2 %slice-start = ((s8[7340032]{0:T(1024)(128)(4,1)}), s8[4194304]{0:T(1024)(128)(4,1)S(1)}, s32[]{:S(2)}) async-start(s8[7340032]{0:T(1024)(128)(4,1)} %bitcast.11), calls=%async_computation.2 | async-start | bytes 8388608
  0.0 41.2 %slice-start.2 = ((s8[7340032]{0:T(1024)(128)(4,1)}), s8[4194304]{0:T(1024)(128)(4,1)S(1)}, s32[]{:S(2)}) async-start(s8[7340032]{0:T(1024)(128)(4,1)} %bitcast.14), calls=%async_computation.4 | async-start | bytes 8388608
  0.0 41.2 %slice-start.4 = ((s8[7340032]{0:T(1024)(128)(4,1)}), s8[4194304]{0:T(1024)(128)(4,1)S(1)}, s32[]{:S(2)}) async-start(s8[7340032]{0:T(1024)(128)(4,1)} %bitcast.17), calls=%async_computation.6 | async-start | bytes 8388608
  0.0 0.8 copy-start
  0.8 1.3 %copy-start.3 = (bf16[16,3584]{1,0:T(8,128)(2,1)S(1)}, bf16[16,3584]{1,0:T(8,128)(2,1)}, u32[]{:S(2)}) copy-start(bf16[16,3584]{1,0:T(8,128)(2,1)} %tokens_ref.1) | copy-start | bytes 344068
  2.2 39.0 %slice-start.1 = ((s8[7340032]{0:T(1024)(128)(4,1)}), s8[3145728]{0:T(1024)(128)(4,1)S(1)}, s32[]{:S(2)}) async-start(s8[7340032]{0:T(1024)(128)(4,1)} %bitcast.11), calls=%async_computation.3 | async-start | bytes 6291456
  2.2 39.0 %slice-start.3 = ((s8[7340032]{0:T(1024)(128)(4,1)}), s8[3145728]{0:T(1024)(128)(4,1)S(1)}, s32[]{:S(2)}) async-start(s8[7340032]{0:T(1024)(128)(4,1)} %bitcast.14), calls=%async_computation.5 | async-start | bytes 6291456
  2.2 39.0 %slice-start.5 = ((s8[7340032]{0:T(1024)(128)(4,1)}), s8[3145728]{0:T(1024)(128)(4,1)S(1)}, s32[]{:S(2)}) async-start(s8[7340032]{0:T(1024)(128)(4,1)} %bitcast.17), calls=%async_computation.7 | async-start | bytes 6291456
  51.6 4.8 %copy-start.1 = (s32[16,8]{0,1:T(8,128)S(1)}, s32[16,8]{0,1:T(8,128)}, u32[]{:S(2)}) copy-start(s32[16,8]{0,1:T(8,128)} %param.7) | copy-start | bytes 1540
  51.7 4.8 %copy-start.2 = (bf16[16,8]{0,1:T(8,128)(2,1)S(1)}, bf16[16,8]{0,1:T(8,128)(2,1)}, u32[]{:S(2)}) copy-start(bf16[16,8]{0,1:T(8,128)(2,1)} %param.8) | copy-start | bytes 772
  51.7 31.9 %all-to-all-start.1 = ((bf16[128,8,896]{2,1,0:T(8,128)(2,1)}), bf16[128,8,896]{2,1,0:T(8,128)(2,1)S(1)}, u32[]{:S(2)}, u32[]{:S(2)}) async-start(bf16[128,8,896]{2,1,0:T(8,128)(2,1)} %bitcast.7), calls=%async_computation.1 | async-start | bytes 3670016 | tf_op jit(solution)/shard_map/all_to_all | solution.py:179

commit v3 on v2

v3 whole, which is shorter than its diff:
```python
import jax
import jax.numpy as jnp
from jax import lax
from jax.experimental import pallas as pl
from jax.experimental.pallas import tpu as pltpu
from jax.sharding import PartitionSpec as P

PAIR = 2
SEGMENTS = 4
BLOCK = PAIR * SEGMENTS
GROUP = 256

MIB = 1 << 20


def routing(ids_t, rows):
    topk, tok_count = ids_t.shape
    experts = rows // BLOCK
    expert = lax.broadcasted_iota(jnp.int32, (experts, tok_count), 0)
    used = jnp.zeros((experts, tok_count), jnp.float32)
    for k in range(topk):
        used = jnp.where(ids_t[k : k + 1, :] == expert, 1.0, used)
    wide = (tok_count, SEGMENTS * tok_count)
    column = lax.broadcasted_iota(jnp.int32, wide, 1) & (tok_count - 1)
    token = lax.broadcasted_iota(jnp.int32, wide, 0)
    weight = jnp.where(token < column, 1.0, jnp.where(token == column, -64.0, 0.0))
    rank = jnp.dot(used.astype(jnp.bfloat16), weight.astype(jnp.bfloat16), preferred_element_type=jnp.float32)
    rank = (rank + 64.0).astype(jnp.int32)
    shape = (experts, BLOCK, SEGMENTS * tok_count)
    rank = jnp.broadcast_to(rank[:, None, :], shape).reshape(rows, SEGMENTS * tok_count)
    row = lax.broadcasted_iota(jnp.int32, rank.shape, 0)
    lane = lax.broadcasted_iota(jnp.int32, rank.shape, 1)
    slot = row & (PAIR - 1)
    segment = (row & (BLOCK - 1)) >> 1
    return (rank == slot) & ((lane >> 4) == segment)


def dispatch_kernel(ids_hbm, tokens_hbm, out_ref, ids_ref, tokens_ref, sems):
    ids_copy = pltpu.make_async_copy(ids_hbm, ids_ref, sems.at[0])
    tokens_copy = pltpu.make_async_copy(tokens_hbm, tokens_ref, sems.at[1])
    ids_copy.start()
    tokens_copy.start()
    rows, width = out_ref.shape
    ids_copy.wait()
    chosen = routing(ids_ref[...], rows)
    chosen = jnp.where(chosen, 1.0, 0.0).astype(jnp.bfloat16)
    tokens_copy.wait()
    table = jnp.concatenate(
        [tokens_ref[:, s * width : (s + 1) * width] for s in range(SEGMENTS)], axis=0
    )
    out_ref[...] = jnp.dot(chosen, table, preferred_element_type=jnp.float32).astype(jnp.bfloat16)


def gate_table(ids_t, gates_t, rows):
    topk, tok_count = ids_t.shape
    experts = rows // BLOCK
    expert = lax.broadcasted_iota(jnp.int32, (experts, tok_count), 0)
    gate = jnp.zeros((experts, tok_count), jnp.float32)
    for k in range(topk):
        gate = jnp.where(ids_t[k : k + 1, :] == expert, gates_t[k : k + 1, :], gate)
    gate = jnp.concatenate([gate] * SEGMENTS, axis=1)
    shape = (experts, BLOCK, SEGMENTS * tok_count)
    gate = jnp.broadcast_to(gate[:, None, :], shape).reshape(rows, SEGMENTS * tok_count)
    return jnp.where(routing(ids_t, rows), gate, 0.0).T.astype(jnp.bfloat16)


def combine_kernel(weights_ref, rows_ref, out_ref):
    tok_count = out_ref.shape[0]
    width = rows_ref.shape[1]
    total = jnp.dot(weights_ref[...], rows_ref[...], preferred_element_type=jnp.float32)
    total = total.astype(jnp.bfloat16)
    for s in range(SEGMENTS):
        out_ref[:, s * width : (s + 1) * width] = total[s * tok_count : (s + 1) * tok_count, :]


def reorder(forward):
    part = GROUP // SEGMENTS
    a = lax.broadcasted_iota(jnp.int32, (GROUP, GROUP), 0 if forward else 1)
    b = lax.broadcasted_iota(jnp.int32, (GROUP, GROUP), 1 if forward else 0)
    inside = a & (part - 1)
    place = (inside >> 1) * BLOCK + (a >> 6) * PAIR + (inside & 1)
    return jnp.where(place == b, 1.0, 0.0).astype(jnp.bfloat16)


def expert_kernel(
    rows_ref, gate_ref, up_ref, down_ref, ids_ref, gates_ref, out_ref, weights_ref, x_ref, h_ref, y_ref
):
    total, width = rows_ref.shape
    part = GROUP // SEGMENTS
    groups = total // GROUP
    hid = gate_ref.shape[1]
    depth = down_ref.shape[1]
    tile = 512
    forward = reorder(True)
    for g in range(groups):
        block = jnp.dot(
            forward, rows_ref[g * GROUP : (g + 1) * GROUP, :], preferred_element_type=jnp.float32
        ).astype(jnp.bfloat16)
        for s in range(SEGMENTS):
            x_ref[g * part : (g + 1) * part, s * width : (s + 1) * width] = block[
                s * part : (s + 1) * part, :
            ]
    for n in range(hid // tile):
        columns = slice(n * tile, (n + 1) * tile)
        gate = jnp.dot(x_ref[...], gate_ref[:, columns], preferred_element_type=jnp.float32)
        upper = jnp.dot(x_ref[...], up_ref[:, columns], preferred_element_type=jnp.float32)
        h_ref[:, columns] = (gate / (1.0 + jnp.exp(-gate)) * upper).astype(jnp.bfloat16)
    weights_ref[...] = gate_table(ids_ref[...], gates_ref[...].astype(jnp.float32), total)
    for n in range(depth // tile):
        columns = slice(n * tile, (n + 1) * tile)
        y_ref[:, columns] = jnp.dot(
            h_ref[...], down_ref[:, columns], preferred_element_type=jnp.float32
        ).astype(jnp.bfloat16)
    back = reorder(False)
    for g in range(groups):
        block = jnp.concatenate(
            [
                y_ref[g * part : (g + 1) * part, s * width : (s + 1) * width]
                for s in range(SEGMENTS)
            ],
            axis=0,
        )
        out_ref[g * GROUP : (g + 1) * GROUP, :] = jnp.dot(
            back, block, preferred_element_type=jnp.float32
        ).astype(jnp.bfloat16)


def exchange(rows, experts, piece):
    blocks = rows.reshape(experts, BLOCK, piece)
    moved = lax.all_to_all(blocks, ("node", "local"), split_axis=0, concat_axis=0, tiled=True)
    return moved.reshape(rows.shape)


def vmem():
    return pl.BlockSpec(memory_space=pltpu.VMEM)


def local(tokens, expert_ids, gate_values, w_gate, w_up, w_down):
    tok_count, width = tokens.shape
    topk = expert_ids.shape[1]
    hid = w_gate.shape[2]
    experts = lax.axis_size("node") * lax.axis_size("local")
    rows = experts * BLOCK
    piece = width // SEGMENTS
    m = experts * PAIR
    bf16 = jnp.bfloat16
    hbm = pl.BlockSpec(memory_space=pltpu.HBM)
    ids_t = expert_ids.T
    outgoing = pl.pallas_call(
        dispatch_kernel,
        out_shape=jax.ShapeDtypeStruct((rows, piece), bf16),
        in_specs=[hbm] * 2,
        out_specs=vmem(),
        scratch_shapes=[
            pltpu.VMEM((topk, tok_count), jnp.int32),
            pltpu.VMEM((tok_count, width), bf16),
            pltpu.SemaphoreType.DMA((2,)),
        ],
        compiler_params=pltpu.CompilerParams(vmem_limit_bytes=12 * MIB),
        cost_estimate=pl.CostEstimate(
            flops=30_000_000_000, bytes_accessed=60_000_000, transcendentals=0
        ),
    )(*(pltpu.with_memory_space_constraint(v, pltpu.HBM) for v in (ids_t, tokens)))
    incoming = exchange(outgoing, experts, piece)
    result, weights = pl.pallas_call(
        expert_kernel,
        out_shape=[
            jax.ShapeDtypeStruct((rows, piece), bf16),
            jax.ShapeDtypeStruct((SEGMENTS * tok_count, rows), bf16),
        ],
        in_specs=[vmem()] * 6,
        out_specs=[vmem()] * 2,
        scratch_shapes=[
            pltpu.VMEM((m, width), bf16),
            pltpu.VMEM((m, hid), bf16),
            pltpu.VMEM((m, width), bf16),
        ],
        compiler_params=pltpu.CompilerParams(vmem_limit_bytes=20 * MIB),
        cost_estimate=pl.CostEstimate(
            flops=6 * m * width * hid, bytes_accessed=6 * width * hid, transcendentals=m * hid
        ),
    )(incoming, w_gate[0], w_up[0], w_down[0], ids_t, gate_values.T)
    answered = exchange(result, experts, piece)
    return pl.pallas_call(
        combine_kernel,
        out_shape=jax.ShapeDtypeStruct((tok_count, width), bf16),
        in_specs=[vmem()] * 2,
        out_specs=vmem(),
        compiler_params=pltpu.CompilerParams(vmem_limit_bytes=12 * MIB),
        cost_estimate=pl.CostEstimate(
            flops=2 * rows * 64 * piece, bytes_accessed=2 * rows * piece, transcendentals=0
        ),
    )(weights, answered)


def solution(mesh):
    return jax.shard_map(
        local,
        mesh=mesh,
        in_specs=(
            P(("node", "local"), None),
            P(("node", "local"), None),
            P(("node", "local"), None),
            P(("node", "local"), None, None),
            P(("node", "local"), None, None),
            P(("node", "local"), None, None),
        ),
        out_specs=P(("node", "local"), None),
        check_vma=False,
    )
```

time: 84.8 us -> 80.4 us (0.948)
  blocking collectives: 38.2 us -> 69.7 us
  waiting for transfers between devices: 26.6 us -> 0 us
  starting transfers between devices: 4.8 us -> 0 us
  Pallas kernels: 12.7 us -> 10.5 us
  local copies, waits for them, and re-layouts: 2.19 us -> 0.04 us
    all_to_all x1 -> x2, blocking collectives: 38.2 us -> 69.7 us  [exchange(): lax.all_to_all(blocks, ('node', 'local'), split_axis=0, concat_axis=0, ti...]
    all_to_all x1 -> x0, waiting for transfers between devices: 26.6 us -> none  [local(): lax.all_to_all(result.reshape(experts, BLOCK, piece), ('node', 'local'),...]
    all_to_all x1 -> x0, starting transfers between devices: 4.8 us -> none  [local(): lax.all_to_all(result.reshape(experts, BLOCK, piece), ('node', 'local'),...]
    pallas_call x4 -> x3, Pallas kernels: 12.7 us -> 10.5 us  [the longest x1 7.46 us: local(): pl.pallas_call(expert_kernel, out_shape=[jax.ShapeDtypeStruct((rows, piec...]
    unnamed x20 -> x16, local copies, waits for them, and re-layouts: 2.19 us -> 0.04 us
  transfers between devices with their start and end apart: 1 -> 0, of which waited for: 1 -> 0; matrix products, arithmetic and copies ran while one was open for 0% -> 0% of each run, Pallas kernels for 1% -> 0%
where the time goes in v3:
time: 80.4 us; the launch traced here: 80.3 us
  blocking collectives  69.7 us (87%)
  Pallas kernels  10.5 us (13%)
    all_to_all x2, blocking collectives, exchange(): lax.all_to_all(blocks, ('node', 'local'), split_axis=0, concat_axis=0, ti...  69.7 us
    pallas_call x1, Pallas kernels, local(): pl.pallas_call(expert_kernel, out_shape=[jax.ShapeDtypeStruct((rows, piec...  7.46 us
    pallas_call x1, Pallas kernels, local(): pl.pallas_call(dispatch_kernel, out_shape=jax.ShapeDtypeStruct((rows, pie...  1.91 us

profile of v3, /device:TPU:1, one launch (start us, length us, event | category | flops | bytes accessed | tf_op | source)
XLA Modules:
  0.0 80.3 jit_solution(7759631965209013696)
XLA Ops:
  0.0 0.0 slice-start
  0.0 0.0 slice-start.2
  0.0 0.0 slice-start.4
  0.0 0.0 slice-start.1
  0.0 0.0 slice-start.3
  0.0 0.0 slice-start.5
  0.0 1.9 %shard_map.64 = bf16[1024,896]{1,0:T(8,128)(2,1)S(1)} custom-call(s32[8,16]{1,0:T(8,128)} %bitcast.22, bf16[16,3584]{1,0:T(8,128)(2,1)} %tokens_hbm.1), custom_call_target="tpu_custom_call" | custom-call | flops 30000001024 | bytes 60000000 | tf_op jit(solution)/shard_map/pallas_call | solution.py:149
  2.0 0.0 copy-start
  2.0 0.0 copy-start.1
  2.0 38.2 %all_to_all.10 = bf16[128,8,896]{2,1,0:T(8,128)(2,1)S(1)} all-to-all(bf16[128,8,896]{2,1,0:T(8,128)(2,1)S(1)} %bitcast.21), channel_id=1, replica_groups=mesh['node'=8,'local'=16] {'node','local'}, dimensions={0} | all-to-all | bytes 3670016 | tf_op jit(solution)/shard_map/all_to_all | solution.py:130
  40.2 0.0 slice-done
  40.2 0.0 slice-done.2
  40.2 0.0 slice-done.4
  40.2 0.0 slice-done.1
  40.2 0.0 slice-done.3
  40.2 0.0 slice-done.5
  40.2 0.0 copy-done
  40.2 0.0 copy-done.1
  40.3 7.5 %shard_map.65 = (bf16[1024,896]{1,0:T(8,128)(2,1)S(1)}, bf16[64,1024]{1,0:T(8,128)(2,1)S(1)}) custom-call(bf16[1024,896]{1,0:T(8,128)(2,1)S(1)} %bitcast.10, bf16[3584,1024]{1,0:T(8,128)(2,1)S(1)} %bitcast.13, bf16[3584,1024]{1,0:T(8,128)(2,1)S(1)} %bitcast.16, bf16[1024,3584]{1,0:T(8,128)(2,1)S(1)} %bitcast.19, s32[8,16]{1,0:T(8,128)S(1)} %bitcast.23, ...), custom_call_target="tpu_custom_call" | custom-call | flops 5637144576 | bytes 22020096 | tf_op jit(solution)/shard_map/pallas_call | solution.py:165
  47.7 31.5 %all_to_all.11 = bf16[128,8,896]{2,1,0:T(8,128)(2,1)S(1)} all-to-all(bf16[128,8,896]{2,1,0:T(8,128)(2,1)S(1)} %bitcast.20), channel_id=1, replica_groups=mesh['node'=8,'local'=16] {'node','local'}, dimensions={0} | all-to-all | bytes 3670016 | tf_op jit(solution)/shard_map/all_to_all | solution.py:130
  79.2 1.1 %shard_map.66 = bf16[16,3584]{1,0:T(8,128)(2,1)} custom-call(bf16[64,1024]{1,0:T(8,128)(2,1)S(1)} %get-tuple-element.7.weights_ref, bf16[1024,896]{1,0:T(8,128)(2,1)S(1)} %bitcast.9), custom_call_target="tpu_custom_call" | custom-call | flops 117440512 | bytes 1835008 | tf_op jit(solution)/shard_map/pallas_call | solution.py:184
  (3 shorter events, 0.0 us)
Async XLA Ops:
  0.0 40.2 %slice-start = ((s8[7340032]{0:T(1024)(128)(4,1)}), s8[4194304]{0:T(1024)(128)(4,1)S(1)}, s32[]{:S(2)}) async-start(s8[7340032]{0:T(1024)(128)(4,1)} %bitcast.11), calls=%async_computation.2 | async-start | bytes 8388608
  0.0 40.2 %slice-start.2 = ((s8[7340032]{0:T(1024)(128)(4,1)}), s8[4194304]{0:T(1024)(128)(4,1)S(1)}, s32[]{:S(2)}) async-start(s8[7340032]{0:T(1024)(128)(4,1)} %bitcast.14), calls=%async_computation.4 | async-start | bytes 8388608
  0.0 40.2 %slice-start.4 = ((s8[7340032]{0:T(1024)(128)(4,1)}), s8[4194304]{0:T(1024)(128)(4,1)S(1)}, s32[]{:S(2)}) async-start(s8[7340032]{0:T(1024)(128)(4,1)} %bitcast.17), calls=%async_computation.6 | async-start | bytes 8388608
  0.0 40.2 %slice-start.1 = ((s8[7340032]{0:T(1024)(128)(4,1)}), s8[3145728]{0:T(1024)(128)(4,1)S(1)}, s32[]{:S(2)}) async-start(s8[7340032]{0:T(1024)(128)(4,1)} %bitcast.11), calls=%async_computation.3 | async-start | bytes 6291456
  0.0 40.2 %slice-start.3 = ((s8[7340032]{0:T(1024)(128)(4,1)}), s8[3145728]{0:T(1024)(128)(4,1)S(1)}, s32[]{:S(2)}) async-start(s8[7340032]{0:T(1024)(128)(4,1)} %bitcast.14), calls=%async_computation.5 | async-start | bytes 6291456
  0.0 40.2 %slice-start.5 = ((s8[7340032]{0:T(1024)(128)(4,1)}), s8[3145728]{0:T(1024)(128)(4,1)S(1)}, s32[]{:S(2)}) async-start(s8[7340032]{0:T(1024)(128)(4,1)} %bitcast.17), calls=%async_computation.7 | async-start | bytes 6291456
  2.0 38.3 %copy-start = (s32[16,8]{0,1:T(8,128)S(1)}, s32[16,8]{0,1:T(8,128)}, u32[]{:S(2)}) copy-start(s32[16,8]{0,1:T(8,128)} %param.7) | copy-start | bytes 1540
  2.0 38.3 %copy-start.1 = (bf16[16,8]{0,1:T(8,128)(2,1)S(1)}, bf16[16,8]{0,1:T(8,128)(2,1)}, u32[]{:S(2)}) copy-start(bf16[16,8]{0,1:T(8,128)(2,1)} %param.8) | copy-start | bytes 772

commit v4 on v0

v4 whole, which is shorter than its diff:
```python
import jax
import jax.numpy as jnp
from jax import lax
from jax.experimental import pallas as pl
from jax.experimental.pallas import tpu as pltpu
from jax.sharding import PartitionSpec as P

PAIR = 2
TILE = 512
MIB = 1 << 20


def routing(ids_t, rows):
    topk, tok_count = ids_t.shape
    row = lax.broadcasted_iota(jnp.int32, (rows, tok_count), 0)
    expert = row >> 1
    used = jnp.zeros((rows, tok_count), jnp.float32)
    for k in range(topk):
        used = jnp.where(ids_t[k : k + 1, :] == expert, 1.0, used)
    column = lax.broadcasted_iota(jnp.int32, (tok_count, tok_count), 1)
    token = lax.broadcasted_iota(jnp.int32, (tok_count, tok_count), 0)
    weight = jnp.where(token < column, 1.0, jnp.where(token == column, -64.0, 0.0))
    rank = jnp.dot(used.astype(jnp.bfloat16), weight.astype(jnp.bfloat16), preferred_element_type=jnp.float32)
    return expert, (rank + 64.0).astype(jnp.int32) == (row & (PAIR - 1))


def dispatch_kernel(ids_hbm, tokens_hbm, out_ref, ids_ref, tokens_ref, sems):
    ids_copy = pltpu.make_async_copy(ids_hbm, ids_ref, sems.at[0])
    tokens_copy = pltpu.make_async_copy(tokens_hbm, tokens_ref, sems.at[1])
    ids_copy.start()
    tokens_copy.start()
    experts, pair, width = out_ref.shape
    ids_copy.wait()
    _, chosen = routing(ids_ref[...], experts * pair)
    chosen = jnp.where(chosen, 1.0, 0.0).astype(jnp.bfloat16)
    tokens_copy.wait()
    for n in range(width // TILE):
        columns = slice(n * TILE, (n + 1) * TILE)
        block = jnp.dot(chosen, tokens_ref[:, columns], preferred_element_type=jnp.float32)
        out_ref[:, :, columns] = block.astype(jnp.bfloat16).reshape(experts, pair, TILE)


def gate_table(ids_t, gates_t, rows):
    expert, chosen = routing(ids_t, rows)
    gate = jnp.zeros(expert.shape, jnp.float32)
    for k in range(ids_t.shape[0]):
        gate = jnp.where(ids_t[k : k + 1, :] == expert, gates_t[k : k + 1, :], gate)
    return jnp.where(chosen, gate, 0.0).T.astype(jnp.bfloat16)


def expert_kernel(rows_ref, gate_ref, up_ref, down_ref, ids_ref, gates_ref, out_ref, table_ref, x_ref, h_ref):
    experts, pair, width = rows_ref.shape
    rows = experts * pair
    hid = gate_ref.shape[1]
    for n in range(width // TILE):
        columns = slice(n * TILE, (n + 1) * TILE)
        x_ref[:, columns] = rows_ref[:, :, columns].reshape(rows, TILE)
    for n in range(hid // TILE):
        columns = slice(n * TILE, (n + 1) * TILE)
        gate = jnp.dot(x_ref[...], gate_ref[:, columns], preferred_element_type=jnp.float32)
        upper = jnp.dot(x_ref[...], up_ref[:, columns], preferred_element_type=jnp.float32)
        h_ref[:, columns] = (gate / (1.0 + jnp.exp(-gate)) * upper).astype(jnp.bfloat16)
    table_ref[...] = gate_table(ids_ref[...], gates_ref[...].astype(jnp.float32), rows)
    for n in range(width // TILE):
        columns = slice(n * TILE, (n + 1) * TILE)
        block = jnp.dot(h_ref[...], down_ref[:, columns], preferred_element_type=jnp.float32)
        out_ref[:, :, columns] = block.astype(jnp.bfloat16).reshape(experts, pair, TILE)


def combine_kernel(table_ref, rows_ref, out_ref):
    experts, pair, width = rows_ref.shape
    for n in range(width // TILE):
        columns = slice(n * TILE, (n + 1) * TILE)
        block = rows_ref[:, :, columns].reshape(experts * pair, TILE)
        total = jnp.dot(table_ref[...], block, preferred_element_type=jnp.float32)
        out_ref[:, columns] = total.astype(jnp.bfloat16)


def exchange(blocks):
    return lax.all_to_all(blocks, ("node", "local"), split_axis=0, concat_axis=0, tiled=True)


def local(tokens, expert_ids, gate_values, w_gate, w_up, w_down):
    tok_count, width = tokens.shape
    topk = expert_ids.shape[1]
    hid = w_gate.shape[2]
    experts = lax.axis_size("node") * lax.axis_size("local")
    rows = experts * PAIR
    bf16 = jnp.bfloat16
    hbm = pl.BlockSpec(memory_space=pltpu.HBM)
    vmem = pl.BlockSpec(memory_space=pltpu.VMEM)
    ids_t = expert_ids.T
    outgoing = pl.pallas_call(
        dispatch_kernel,
        out_shape=jax.ShapeDtypeStruct((experts, PAIR, width), bf16),
        in_specs=[hbm] * 2,
        out_specs=vmem,
        scratch_shapes=[
            pltpu.VMEM((topk, tok_count), jnp.int32),
            pltpu.VMEM((tok_count, width), bf16),
            pltpu.SemaphoreType.DMA((2,)),
        ],
        compiler_params=pltpu.CompilerParams(vmem_limit_bytes=12 * MIB),
        cost_estimate=pl.CostEstimate(
            flops=30_000_000_000, bytes_accessed=60_000_000, transcendentals=0
        ),
    )(*(pltpu.with_memory_space_constraint(v, pltpu.HBM) for v in (ids_t, tokens)))
    incoming = exchange(outgoing)
    result, table = pl.pallas_call(
        expert_kernel,
        out_shape=[
            jax.ShapeDtypeStruct((experts, PAIR, width), bf16),
            jax.ShapeDtypeStruct((tok_count, rows), bf16),
        ],
        in_specs=[vmem] * 6,
        out_specs=[vmem] * 2,
        scratch_shapes=[pltpu.VMEM((rows, width), bf16), pltpu.VMEM((rows, hid), bf16)],
        compiler_params=pltpu.CompilerParams(vmem_limit_bytes=20 * MIB),
        cost_estimate=pl.CostEstimate(
            flops=6 * rows * width * hid, bytes_accessed=6 * width * hid, transcendentals=rows * hid
        ),
    )(incoming, w_gate[0], w_up[0], w_down[0], ids_t, gate_values.T)
    answered = exchange(result)
    return pl.pallas_call(
        combine_kernel,
        out_shape=jax.ShapeDtypeStruct((tok_count, width), bf16),
        in_specs=[vmem] * 2,
        out_specs=vmem,
        compiler_params=pltpu.CompilerParams(vmem_limit_bytes=12 * MIB),
        cost_estimate=pl.CostEstimate(
            flops=2 * rows * tok_count * width, bytes_accessed=2 * rows * width, transcendentals=0
        ),
    )(table, answered)


def solution(mesh):
    return jax.shard_map(
        local,
        mesh=mesh,
        in_specs=(
            P(("node", "local"), None),
            P(("node", "local"), None),
            P(("node", "local"), None),
            P(("node", "local"), None, None),
            P(("node", "local"), None, None),
            P(("node", "local"), None, None),
        ),
        out_specs=P(("node", "local"), None),
        check_vma=False,
    )
```

time: 110 us -> 78.9 us (0.72)
  blocking collectives: 38.2 us -> 69.7 us
  waiting for transfers between devices: 26.6 us -> 0 us
  local copies, waits for them, and re-layouts: 17.2 us -> 0.04 us
  matrix products: 16.4 us -> 0 us
  Pallas kernels: 0 us -> 8.96 us
  starting transfers between devices: 5.82 us -> 0 us
  other arithmetic: 5.18 us -> 0.01 us
    all_to_all x1 -> x2, blocking collectives: 38.2 us -> 69.7 us  [exchange(): lax.all_to_all(blocks, ('node', 'local'), split_axis=0, concat_axis=0, ti...]
    all_to_all x1 -> x0, waiting for transfers between devices: 26.6 us -> none  [local(): lax.all_to_all(result, ('node', 'local'), split_axis=0, concat_axis=0, ti...]
    dot_general x2 -> x0, matrix products: 16.4 us -> none  [the longest x1 10.6 us: expert_rows(): jnp.dot(hidden, w_down[0], preferred_element_type=jnp.float32)]
    reshape x5 -> x0, local copies, waits for them, and re-layouts: 10.7 us -> none  [the longest x1 4.79 us: local(): result = expert_rows(shaped, w_gate, w_up, w_down).reshape(incoming.shape)]
    pallas_call x0 -> x3, Pallas kernels: none -> 8.96 us  [the longest x1 6.23 us: local(): pl.pallas_call(expert_kernel, out_shape=[jax.ShapeDtypeStruct((experts, P...]
    all_to_all x1 -> x0, starting transfers between devices: 5.82 us -> none  [local(): lax.all_to_all(result, ('node', 'local'), split_axis=0, concat_axis=0, ti...]
    gather x3 -> x0, local copies, waits for them, and re-layouts: 4.52 us -> none  [the longest x2 3.41 us: local(): tokens[jnp.maximum(source, 0)]]
    select_n x2 -> x0, other arithmetic: 3.26 us -> none  [the longest x1 3.26 us: local(): jnp.where((source >= 0)[:, None], tokens[jnp.maximum(source, 0)], nothing)]
  transfers between devices with their start and end apart: 1 -> 0, of which waited for: 1 -> 0; matrix products, arithmetic and copies ran while one was open for 0% -> 0% of each run, Pallas kernels for 0% -> 0%
where the time goes in v4:
time: 78.9 us; the launch traced here: 78.8 us
  blocking collectives  69.7 us (88%)
  Pallas kernels  8.96 us (11%)
    all_to_all x2, blocking collectives, exchange(): lax.all_to_all(blocks, ('node', 'local'), split_axis=0, concat_axis=0, ti...  69.7 us
    pallas_call x1, Pallas kernels, local(): pl.pallas_call(expert_kernel, out_shape=[jax.ShapeDtypeStruct((experts, P...  6.23 us
    pallas_call x1, Pallas kernels, local(): pl.pallas_call(dispatch_kernel, out_shape=jax.ShapeDtypeStruct((experts,...  1.7 us

profile of v4, /device:TPU:1, one launch (start us, length us, event | category | flops | bytes accessed | tf_op | source)
XLA Modules:
  0.0 78.8 jit_solution(8657588124215097305)
XLA Ops:
  0.0 0.0 slice-start
  0.0 0.0 slice-start.2
  0.0 0.0 slice-start.4
  0.0 0.0 slice-start.1
  0.0 0.0 slice-start.3
  0.0 0.0 slice-start.5
  0.0 1.7 %shard_map.64 = bf16[128,2,3584]{2,1,0:T(2,128)(2,1)S(1)} custom-call(s32[8,16]{1,0:T(8,128)} %bitcast.14, bf16[16,3584]{1,0:T(8,128)(2,1)} %tokens_hbm.1), custom_call_target="tpu_custom_call" | custom-call | flops 30000001024 | bytes 60000000 | tf_op jit(solution)/shard_map/pallas_call | solution.py:93
  1.7 0.0 copy-start
  1.8 0.0 copy-start.1
  1.8 38.2 %all_to_all.10.rows_ref = bf16[128,2,3584]{2,1,0:T(2,128)(2,1)S(1)} all-to-all(bf16[128,2,3584]{2,1,0:T(2,128)(2,1)S(1)} %shard_map.64), channel_id=1, replica_groups=mesh['node'=8,'local'=16] {'node','local'}, dimensions={0} | all-to-all | bytes 3670016 | tf_op jit(solution)/shard_map/all_to_all | solution.py:80
  40.0 0.0 slice-done
  40.0 0.0 slice-done.2
  40.0 0.0 slice-done.4
  40.0 0.0 slice-done.1
  40.0 0.0 slice-done.3
  40.0 0.0 slice-done.5
  40.0 0.0 copy-done
  40.0 0.0 copy-done.1
  40.1 6.2 %shard_map.65 = (bf16[128,2,3584]{2,1,0:T(2,128)(2,1)S(1)}, bf16[16,256]{1,0:T(8,128)(2,1)S(1)}) custom-call(bf16[128,2,3584]{2,1,0:T(2,128)(2,1)S(1)} %all_to_all.10.rows_ref, bf16[3584,1024]{1,0:T(8,128)(2,1)S(1)} %bitcast.7, bf16[3584,1024]{1,0:T(8,128)(2,1)S(1)} %bitcast.10, bf16[1024,3584]{1,0:T(8,128)(2,1)S(1)} %bitcast.13, s32[8,16]{1,0:T(8,128)S(1)} %bitcast.15, ...), custom_call_target="tpu_custom_call" | custom-call | flops 5637144576 | bytes 22020096 | tf_op jit(solution)/shard_map/pallas_call | solution.py:109
  46.3 31.5 %all_to_all.11.rows_ref = bf16[128,2,3584]{2,1,0:T(2,128)(2,1)S(1)} all-to-all(bf16[128,2,3584]{2,1,0:T(2,128)(2,1)S(1)} %get-tuple-element.8), channel_id=1, replica_groups=mesh['node'=8,'local'=16] {'node','local'}, dimensions={0} | all-to-all | bytes 3670016 | tf_op jit(solution)/shard_map/all_to_all | solution.py:80
  77.8 1.0 %shard_map.66 = bf16[16,3584]{1,0:T(8,128)(2,1)} custom-call(bf16[16,256]{1,0:T(8,128)(2,1)S(1)} %get-tuple-element.7.table_ref, bf16[128,2,3584]{2,1,0:T(2,128)(2,1)S(1)} %all_to_all.11.rows_ref), custom_call_target="tpu_custom_call" | custom-call | flops 29360128 | bytes 1835008 | tf_op jit(solution)/shard_map/pallas_call | solution.py:124
  (3 shorter events, 0.0 us)
Async XLA Ops:
  0.0 40.0 %slice-start = ((s8[7340032]{0:T(1024)(128)(4,1)}), s8[4194304]{0:T(1024)(128)(4,1)S(1)}, s32[]{:S(2)}) async-start(s8[7340032]{0:T(1024)(128)(4,1)} %bitcast.5), calls=%async_computation.2 | async-start | bytes 8388608
  0.0 40.0 %slice-start.2 = ((s8[7340032]{0:T(1024)(128)(4,1)}), s8[4194304]{0:T(1024)(128)(4,1)S(1)}, s32[]{:S(2)}) async-start(s8[7340032]{0:T(1024)(128)(4,1)} %bitcast.8), calls=%async_computation.4 | async-start | bytes 8388608
  0.0 40.0 %slice-start.4 = ((s8[7340032]{0:T(1024)(128)(4,1)}), s8[4194304]{0:T(1024)(128)(4,1)S(1)}, s32[]{:S(2)}) async-start(s8[7340032]{0:T(1024)(128)(4,1)} %bitcast.11), calls=%async_computation.6 | async-start | bytes 8388608
  0.0 40.0 %slice-start.1 = ((s8[7340032]{0:T(1024)(128)(4,1)}), s8[3145728]{0:T(1024)(128)(4,1)S(1)}, s32[]{:S(2)}) async-start(s8[7340032]{0:T(1024)(128)(4,1)} %bitcast.5), calls=%async_computation.3 | async-start | bytes 6291456
  0.0 40.0 %slice-start.3 = ((s8[7340032]{0:T(1024)(128)(4,1)}), s8[3145728]{0:T(1024)(128)(4,1)S(1)}, s32[]{:S(2)}) async-start(s8[7340032]{0:T(1024)(128)(4,1)} %bitcast.8), calls=%async_computation.5 | async-start | bytes 6291456
  0.0 40.0 %slice-start.5 = ((s8[7340032]{0:T(1024)(128)(4,1)}), s8[3145728]{0:T(1024)(128)(4,1)S(1)}, s32[]{:S(2)}) async-start(s8[7340032]{0:T(1024)(128)(4,1)} %bitcast.11), calls=%async_computation.7 | async-start | bytes 6291456
  1.7 38.3 %copy-start = (s32[16,8]{0,1:T(8,128)S(1)}, s32[16,8]{0,1:T(8,128)}, u32[]{:S(2)}) copy-start(s32[16,8]{0,1:T(8,128)} %param.7) | copy-start | bytes 1540
  1.8 38.3 %copy-start.1 = (bf16[16,8]{0,1:T(8,128)(2,1)S(1)}, bf16[16,8]{0,1:T(8,128)(2,1)}, u32[]{:S(2)}) copy-start(bf16[16,8]{0,1:T(8,128)(2,1)} %param.8) | copy-start | bytes 772

commit v5 on v4

--- a/solution.py
+++ b/solution.py
@@ -21,7 +21,7 @@
     token = lax.broadcasted_iota(jnp.int32, (tok_count, tok_count), 0)
     weight = jnp.where(token < column, 1.0, jnp.where(token == column, -64.0, 0.0))
     rank = jnp.dot(used.astype(jnp.bfloat16), weight.astype(jnp.bfloat16), preferred_element_type=jnp.float32)
-    return expert, (rank + 64.0).astype(jnp.int32) == (row & (PAIR - 1))
+    return (rank + 64.0).astype(jnp.int32) == (row & (PAIR - 1))
 
 
 def dispatch_kernel(ids_hbm, tokens_hbm, out_ref, ids_ref, tokens_ref, sems):
@@ -31,7 +31,7 @@
     tokens_copy.start()
     experts, pair, width = out_ref.shape
     ids_copy.wait()
-    _, chosen = routing(ids_ref[...], experts * pair)
+    chosen = routing(ids_ref[...], experts * pair)
     chosen = jnp.where(chosen, 1.0, 0.0).astype(jnp.bfloat16)
     tokens_copy.wait()
     for n in range(width // TILE):
@@ -41,11 +41,23 @@
 
 
 def gate_table(ids_t, gates_t, rows):
-    expert, chosen = routing(ids_t, rows)
-    gate = jnp.zeros(expert.shape, jnp.float32)
-    for k in range(ids_t.shape[0]):
-        gate = jnp.where(ids_t[k : k + 1, :] == expert, gates_t[k : k + 1, :], gate)
-    return jnp.where(chosen, gate, 0.0).T.astype(jnp.bfloat16)
+    topk, tok_count = ids_t.shape
+    ids = ids_t.astype(jnp.float32).T
+    gates = gates_t.T
+    column = lax.broadcasted_iota(jnp.int32, (tok_count, rows), 1)
+    expert = (column >> 1).astype(jnp.float32)
+    gate = jnp.zeros((tok_count, rows), jnp.float32)
+    used = jnp.zeros((tok_count, rows), jnp.float32)
+    for k in range(topk):
+        hit = ids[:, k : k + 1] == expert
+        gate = jnp.where(hit, gates[:, k : k + 1], gate)
+        used = jnp.where(hit, 1.0, used)
+    token = lax.broadcasted_iota(jnp.int32, (tok_count, tok_count), 0)
+    other = lax.broadcasted_iota(jnp.int32, (tok_count, tok_count), 1)
+    weight = jnp.where(other < token, 1.0, jnp.where(other == token, -64.0, 0.0))
+    rank = jnp.dot(weight.astype(jnp.bfloat16), used.astype(jnp.bfloat16), preferred_element_type=jnp.float32)
+    chosen = (rank + 64.0).astype(jnp.int32) == (column & (PAIR - 1))
+    return jnp.where(chosen, gate, 0.0).astype(jnp.bfloat16)
 
 
 def expert_kernel(rows_ref, gate_ref, up_ref, down_ref, ids_ref, gates_ref, out_ref, table_ref, x_ref, h_ref):

time: 78.9 us -> 78.9 us (level)
  no operation moved by 1% of the time
where the time goes in v5:
time: 78.9 us; the launch traced here: 78.8 us
  blocking collectives  69.7 us (88%)
  Pallas kernels  8.95 us (11%)
    all_to_all x2, blocking collectives, exchange(): lax.all_to_all(blocks, ('node', 'local'), split_axis=0, concat_axis=0, ti...  69.7 us
    pallas_call x1, Pallas kernels, local(): pl.pallas_call(expert_kernel, out_shape=[jax.ShapeDtypeStruct((experts, P...  6.22 us
    pallas_call x1, Pallas kernels, local(): pl.pallas_call(dispatch_kernel, out_shape=jax.ShapeDtypeStruct((experts,...  1.7 us

profile of v5, /device:TPU:1, one launch (start us, length us, event | category | flops | bytes accessed | tf_op | source)
XLA Modules:
  0.0 78.8 jit_solution(11187619195746036588)
XLA Ops:
  0.0 0.0 slice-start
  0.0 0.0 slice-start.2
  0.0 0.0 slice-start.4
  0.0 0.0 slice-start.1
  0.0 0.0 slice-start.3
  0.0 0.0 slice-start.5
  0.0 1.7 %shard_map.64 = bf16[128,2,3584]{2,1,0:T(2,128)(2,1)S(1)} custom-call(s32[8,16]{1,0:T(8,128)} %bitcast.14, bf16[16,3584]{1,0:T(8,128)(2,1)} %tokens_hbm.1), custom_call_target="tpu_custom_call" | custom-call | flops 30000001024 | bytes 60000000 | tf_op jit(solution)/shard_map/pallas_call | solution.py:105
  1.7 0.0 copy-start
  1.8 0.0 copy-start.1
  1.8 38.2 %all_to_all.10.rows_ref = bf16[128,2,3584]{2,1,0:T(2,128)(2,1)S(1)} all-to-all(bf16[128,2,3584]{2,1,0:T(2,128)(2,1)S(1)} %shard_map.64), channel_id=1, replica_groups=mesh['node'=8,'local'=16] {'node','local'}, dimensions={0} | all-to-all | bytes 3670016 | tf_op jit(solution)/shard_map/all_to_all | solution.py:92
  40.0 0.0 slice-done
  40.0 0.0 slice-done.2
  40.0 0.0 slice-done.4
  40.0 0.0 slice-done.1
  40.0 0.0 slice-done.3
  40.0 0.0 slice-done.5
  40.0 0.0 copy-done
  40.0 0.0 copy-done.1
  40.1 6.2 %shard_map.65 = (bf16[128,2,3584]{2,1,0:T(2,128)(2,1)S(1)}, bf16[16,256]{1,0:T(8,128)(2,1)S(1)}) custom-call(bf16[128,2,3584]{2,1,0:T(2,128)(2,1)S(1)} %all_to_all.10.rows_ref, bf16[3584,1024]{1,0:T(8,128)(2,1)S(1)} %bitcast.7, bf16[3584,1024]{1,0:T(8,128)(2,1)S(1)} %bitcast.10, bf16[1024,3584]{1,0:T(8,128)(2,1)S(1)} %bitcast.13, s32[8,16]{1,0:T(8,128)S(1)} %bitcast.15, ...), custom_call_target="tpu_custom_call" | custom-call | flops 5637144576 | bytes 22020096 | tf_op jit(solution)/shard_map/pallas_call | solution.py:121
  46.3 31.5 %all_to_all.11.rows_ref = bf16[128,2,3584]{2,1,0:T(2,128)(2,1)S(1)} all-to-all(bf16[128,2,3584]{2,1,0:T(2,128)(2,1)S(1)} %get-tuple-element.8), channel_id=1, replica_groups=mesh['node'=8,'local'=16] {'node','local'}, dimensions={0} | all-to-all | bytes 3670016 | tf_op jit(solution)/shard_map/all_to_all | solution.py:92
  77.8 1.0 %shard_map.66 = bf16[16,3584]{1,0:T(8,128)(2,1)} custom-call(bf16[16,256]{1,0:T(8,128)(2,1)S(1)} %get-tuple-element.7.table_ref, bf16[128,2,3584]{2,1,0:T(2,128)(2,1)S(1)} %all_to_all.11.rows_ref), custom_call_target="tpu_custom_call" | custom-call | flops 29360128 | bytes 1835008 | tf_op jit(solution)/shard_map/pallas_call | solution.py:136
  (3 shorter events, 0.0 us)
Async XLA Ops:
  0.0 40.0 %slice-start = ((s8[7340032]{0:T(1024)(128)(4,1)}), s8[4194304]{0:T(1024)(128)(4,1)S(1)}, s32[]{:S(2)}) async-start(s8[7340032]{0:T(1024)(128)(4,1)} %bitcast.5), calls=%async_computation.2 | async-start | bytes 8388608
  0.0 40.0 %slice-start.2 = ((s8[7340032]{0:T(1024)(128)(4,1)}), s8[4194304]{0:T(1024)(128)(4,1)S(1)}, s32[]{:S(2)}) async-start(s8[7340032]{0:T(1024)(128)(4,1)} %bitcast.8), calls=%async_computation.4 | async-start | bytes 8388608
  0.0 40.0 %slice-start.4 = ((s8[7340032]{0:T(1024)(128)(4,1)}), s8[4194304]{0:T(1024)(128)(4,1)S(1)}, s32[]{:S(2)}) async-start(s8[7340032]{0:T(1024)(128)(4,1)} %bitcast.11), calls=%async_computation.6 | async-start | bytes 8388608
  0.0 40.0 %slice-start.1 = ((s8[7340032]{0:T(1024)(128)(4,1)}), s8[3145728]{0:T(1024)(128)(4,1)S(1)}, s32[]{:S(2)}) async-start(s8[7340032]{0:T(1024)(128)(4,1)} %bitcast.5), calls=%async_computation.3 | async-start | bytes 6291456
  0.0 40.0 %slice-start.3 = ((s8[7340032]{0:T(1024)(128)(4,1)}), s8[3145728]{0:T(1024)(128)(4,1)S(1)}, s32[]{:S(2)}) async-start(s8[7340032]{0:T(1024)(128)(4,1)} %bitcast.8), calls=%async_computation.5 | async-start | bytes 6291456
  0.0 40.0 %slice-start.5 = ((s8[7340032]{0:T(1024)(128)(4,1)}), s8[3145728]{0:T(1024)(128)(4,1)S(1)}, s32[]{:S(2)}) async-start(s8[7340032]{0:T(1024)(128)(4,1)} %bitcast.11), calls=%async_computation.7 | async-start | bytes 6291456
  1.7 38.3 %copy-start = (s32[16,8]{0,1:T(8,128)S(1)}, s32[16,8]{0,1:T(8,128)}, u32[]{:S(2)}) copy-start(s32[16,8]{0,1:T(8,128)} %param.7) | copy-start | bytes 1540
  1.8 38.3 %copy-start.1 = (bf16[16,8]{0,1:T(8,128)(2,1)S(1)}, bf16[16,8]{0,1:T(8,128)(2,1)}, u32[]{:S(2)}) copy-start(bf16[16,8]{0,1:T(8,128)(2,1)} %param.8) | copy-start | bytes 772

commit v6 on v4

v6 whole, which is shorter than its diff:
```python
import jax
import jax.numpy as jnp
from jax import lax
from jax.experimental import pallas as pl
from jax.experimental.pallas import tpu as pltpu
from jax.sharding import PartitionSpec as P

PAIR = 2
TILE = 512
MIB = 1 << 20


CORES = 2


def expert_of(index, core, width):
    return (index // width) * (CORES * width) + core * width + (index & (width - 1))


def ranks(used):
    count = used.shape[1]
    column = lax.broadcasted_iota(jnp.int32, (count, count), 1)
    token = lax.broadcasted_iota(jnp.int32, (count, count), 0)
    weight = jnp.where(token < column, 1.0, jnp.where(token == column, -64.0, 0.0))
    rank = jnp.dot(used.astype(jnp.bfloat16), weight.astype(jnp.bfloat16), preferred_element_type=jnp.float32)
    return (rank + 64.0).astype(jnp.int32)


def dispatch_kernel(ids_ref, tokens_ref, out_ref):
    chips, block, width = out_ref.shape
    rows = chips * block
    tok_count = tokens_ref.shape[0]
    topk = ids_ref.shape[0] // CORES
    core = lax.axis_index("core")
    places = lax.axis_size("local")
    row = lax.broadcasted_iota(jnp.int32, (rows, tok_count), 0)
    column = lax.broadcasted_iota(jnp.int32, (rows, tok_count), 1)
    expert = jnp.where(
        ((row >> 1) & 1) == column // (tok_count // CORES), expert_of(row >> 2, core, places), -1
    )
    ids = jnp.concatenate([ids_ref[c * topk : (c + 1) * topk, :] for c in range(CORES)], axis=1)
    used = jnp.zeros((rows, tok_count), jnp.float32)
    for k in range(topk):
        used = jnp.where(ids[k : k + 1, :] == expert, 1.0, used)
    chosen = jnp.where(ranks(used) == (row & (PAIR - 1)), 1.0, 0.0).astype(jnp.bfloat16)
    for n in range(width // TILE):
        columns = slice(n * TILE, (n + 1) * TILE)
        total = jnp.dot(chosen, tokens_ref[:, columns], preferred_element_type=jnp.float32)
        out_ref[:, :, columns] = total.astype(jnp.bfloat16).reshape(chips, block, TILE)


def gate_table(ids_t, gates_t, rows):
    topk, tok_count = ids_t.shape
    row = lax.broadcasted_iota(jnp.int32, (rows, tok_count), 0)
    expert = expert_of(row >> 2, (row >> 1) & 1, lax.axis_size("local"))
    used = jnp.zeros((rows, tok_count), jnp.float32)
    gate = jnp.zeros((rows, tok_count), jnp.float32)
    for k in range(topk):
        hit = ids_t[k : k + 1, :] == expert
        used = jnp.where(hit, 1.0, used)
        gate = jnp.where(hit, gates_t[k : k + 1, :], gate)
    return jnp.where(ranks(used) == (row & (PAIR - 1)), gate, 0.0).T.astype(jnp.bfloat16)


def expert_kernel(rows_ref, gate_ref, up_ref, down_ref, ids_ref, gates_ref, out_ref, table_ref, x_ref, h_ref):
    experts, pair, width = out_ref.shape
    rows = experts * pair
    hid = gate_ref.shape[1]
    for n in range(width // TILE):
        columns = slice(n * TILE, (n + 1) * TILE)
        x_ref[:, columns] = rows_ref[:, :, columns].reshape(rows, TILE)
    for n in range(hid // TILE):
        columns = slice(n * TILE, (n + 1) * TILE)
        gate = jnp.dot(x_ref[...], gate_ref[:, columns], preferred_element_type=jnp.float32)
        upper = jnp.dot(x_ref[...], up_ref[:, columns], preferred_element_type=jnp.float32)
        h_ref[:, columns] = (gate / (1.0 + jnp.exp(-gate)) * upper).astype(jnp.bfloat16)
    table_ref[...] = gate_table(ids_ref[...], gates_ref[...].astype(jnp.float32), rows)
    for n in range(width // TILE):
        columns = slice(n * TILE, (n + 1) * TILE)
        block = jnp.dot(h_ref[...], down_ref[:, columns], preferred_element_type=jnp.float32)
        out_ref[:, :, columns] = block.astype(jnp.bfloat16).reshape(experts, pair, TILE)


def combine_kernel(table_ref, rows_ref, out_ref):
    experts, pair, width = rows_ref.shape
    for n in range(width // TILE):
        columns = slice(n * TILE, (n + 1) * TILE)
        block = rows_ref[:, :, columns].reshape(experts * pair, TILE)
        total = jnp.dot(table_ref[...], block, preferred_element_type=jnp.float32)
        out_ref[:, columns] = total.astype(jnp.bfloat16)


def exchange(blocks, axes):
    return lax.all_to_all(blocks, axes, split_axis=0, concat_axis=0, tiled=True)


def local(tokens, expert_ids, gate_values, w_gate, w_up, w_down):
    tok_count, width = tokens.shape
    hid = w_gate.shape[2]
    chips = lax.axis_size("z") * lax.axis_size("local")
    experts = chips * CORES
    rows = experts * PAIR
    bf16 = jnp.bfloat16
    vmem = pl.BlockSpec(memory_space=pltpu.VMEM)
    ids_t = expert_ids.T
    both_ids = lax.all_gather(ids_t, "core", axis=0, tiled=True)
    both_tokens = lax.all_gather(tokens, "core", axis=0, tiled=True)
    outgoing = pl.pallas_call(
        dispatch_kernel,
        out_shape=jax.ShapeDtypeStruct((chips, CORES * PAIR, width), bf16),
        in_specs=[vmem] * 2,
        out_specs=vmem,
        compiler_params=pltpu.CompilerParams(vmem_limit_bytes=12 * MIB),
        cost_estimate=pl.CostEstimate(
            flops=30_000_000_000, bytes_accessed=60_000_000, transcendentals=0
        ),
    )(both_ids, both_tokens)
    incoming = exchange(outgoing, ("z", "local"))
    result, table = pl.pallas_call(
        expert_kernel,
        out_shape=[
            jax.ShapeDtypeStruct((experts, PAIR, width), bf16),
            jax.ShapeDtypeStruct((tok_count, rows), bf16),
        ],
        in_specs=[vmem] * 6,
        out_specs=[vmem] * 2,
        scratch_shapes=[pltpu.VMEM((rows, width), bf16), pltpu.VMEM((rows, hid), bf16)],
        compiler_params=pltpu.CompilerParams(vmem_limit_bytes=20 * MIB),
        cost_estimate=pl.CostEstimate(
            flops=6 * rows * width * hid, bytes_accessed=6 * width * hid, transcendentals=rows * hid
        ),
    )(incoming, w_gate[0], w_up[0], w_down[0], ids_t, gate_values.T)
    answered = exchange(result, ("z", "local", "core"))
    return pl.pallas_call(
        combine_kernel,
        out_shape=jax.ShapeDtypeStruct((tok_count, width), bf16),
        in_specs=[vmem] * 2,
        out_specs=vmem,
        compiler_params=pltpu.CompilerParams(vmem_limit_bytes=12 * MIB),
        cost_estimate=pl.CostEstimate(
            flops=2 * rows * tok_count * width, bytes_accessed=2 * rows * width, transcendentals=0
        ),
    )(table, answered)


def solution(mesh):
    nodes, places = mesh.devices.shape
    devices = mesh.devices.reshape(nodes // CORES, CORES, places)
    axes = ("z", "core", "local")
    flat = P(axes, None)
    whole = P(axes, None, None)
    return jax.shard_map(
        local,
        mesh=jax.sharding.Mesh(devices, axes),
        in_specs=(flat, flat, flat, whole, whole, whole),
        out_specs=flat,
        check_vma=False,
    )
```

time: 78.9 us -> 84.8 us (1.075)
  blocking collectives: 69.7 us -> 76.5 us
  Pallas kernels: 8.96 us -> 8 us
    all_gather x0 -> x2, blocking collectives: none -> 5.34 us  [the longest x1 3.04 us: local(): both_ids = lax.all_gather(ids_t, 'core', axis=0, tiled=True)]
    all_to_all x2, blocking collectives: 69.7 us -> 71.2 us  [exchange(): return lax.all_to_all(blocks, axes, split_axis=0, concat_axis=0, tiled=True)]
where the time goes in v6:
time: 84.8 us; the launch traced here: 84.6 us
  blocking collectives  76.5 us (90%)
  Pallas kernels  8 us (9%)
    all_to_all x2, blocking collectives, exchange(): return lax.all_to_all(blocks, axes, split_axis=0, concat_axis=0, tiled=True)  71.2 us
    pallas_call x1, Pallas kernels, local(): pl.pallas_call(expert_kernel, out_shape=[jax.ShapeDtypeStruct((experts, P...  6.05 us
    all_gather x1, blocking collectives, local(): both_ids = lax.all_gather(ids_t, 'core', axis=0, tiled=True)  3.04 us
    all_gather x1, blocking collectives, local(): both_tokens = lax.all_gather(tokens, 'core', axis=0, tiled=True)  2.3 us

profile of v6, /device:TPU:1, one launch (start us, length us, event | category | flops | bytes accessed | tf_op | source)
XLA Modules:
  0.0 84.6 jit_solution(8377994691296690028)
XLA Ops:
  0.0 3.0 %all_gather.6.ids_ref = s32[16,16]{1,0:T(8,128)S(1)} all-gather(s32[8,16]{1,0:T(8,128)} %bitcast.14), channel_id=1, replica_groups=mesh['z'=4,'core'=2,'local'=16] {'core'}, dimensions={0}, use_global_device_ids=true | all-gather | bytes 1536 | tf_op jit(solution)/shard_map/all_gather | solution.py:106
  3.0 0.0 slice-start
  3.0 0.0 slice-start.2
  3.0 0.0 slice-start.4
  3.0 2.3 %all_gather.7.tokens_ref = bf16[32,3584]{1,0:T(8,128)(2,1)S(1)} all-gather(bf16[16,3584]{1,0:T(8,128)(2,1)} %param.6), channel_id=1, replica_groups=mesh['z'=4,'core'=2,'local'=16] {'core'}, dimensions={0}, use_global_device_ids=true | all-gather | bytes 344064 | tf_op jit(solution)/shard_map/all_gather | solution.py:107
  5.3 0.0 slice-start.1
  5.3 0.0 slice-start.3
  5.3 0.0 slice-start.5
  5.4 0.9 %shard_map.64 = bf16[64,4,3584]{2,1,0:T(4,128)(2,1)S(1)} custom-call(s32[16,16]{1,0:T(8,128)S(1)} %all_gather.6.ids_ref, bf16[32,3584]{1,0:T(8,128)(2,1)S(1)} %all_gather.7.tokens_ref), custom_call_target="tpu_custom_call" | custom-call | flops 30000001024 | bytes 60000000 | tf_op jit(solution)/shard_map/pallas_call | solution.py:108
  6.3 0.0 copy-start
  6.3 0.0 copy-start.1
  6.3 37.5 %all_to_all.10.rows_ref = bf16[64,4,3584]{2,1,0:T(4,128)(2,1)S(1)} all-to-all(bf16[64,4,3584]{2,1,0:T(4,128)(2,1)S(1)} %shard_map.64), channel_id=1, replica_groups=mesh['z'=4,'core'=2,'local'=16] {'z','local'}, dimensions={0} | all-to-all | bytes 3670016 | tf_op jit(solution)/shard_map/all_to_all | solution.py:94
  43.8 0.0 slice-done
  43.8 0.0 slice-done.2
  43.8 0.0 slice-done.4
  43.8 0.0 slice-done.1
  43.8 0.0 slice-done.3
  43.8 0.0 slice-done.5
  43.8 0.0 copy-done
  43.8 0.0 copy-done.1
  43.9 6.1 %shard_map.65 = (bf16[128,2,3584]{2,1,0:T(2,128)(2,1)S(1)}, bf16[16,256]{1,0:T(8,128)(2,1)S(1)}) custom-call(bf16[64,4,3584]{2,1,0:T(4,128)(2,1)S(1)} %all_to_all.10.rows_ref, bf16[3584,1024]{1,0:T(8,128)(2,1)S(1)} %bitcast.7, bf16[3584,1024]{1,0:T(8,128)(2,1)S(1)} %bitcast.10, bf16[1024,3584]{1,0:T(8,128)(2,1)S(1)} %bitcast.13, s32[8,16]{1,0:T(8,128)S(1)} %bitcast.15, ...), custom_call_target="tpu_custom_call" | custom-call | flops 5637144576 | bytes 22020096 | tf_op jit(solution)/shard_map/pallas_call | solution.py:119
  49.9 33.7 %all_to_all.11.rows_ref = bf16[128,2,3584]{2,1,0:T(2,128)(2,1)S(1)} all-to-all(bf16[128,2,3584]{2,1,0:T(2,128)(2,1)S(1)} %get-tuple-element.8), channel_id=1, replica_groups=mesh['z'=4,'core'=2,'local'=16] {'z','local','core'}, dimensions={0} | all-to-all | bytes 3670016 | tf_op jit(solution)/shard_map/all_to_all | solution.py:94
  83.6 1.0 %shard_map.66 = bf16[16,3584]{1,0:T(8,128)(2,1)} custom-call(bf16[16,256]{1,0:T(8,128)(2,1)S(1)} %get-tuple-element.7.table_ref, bf16[128,2,3584]{2,1,0:T(2,128)(2,1)S(1)} %all_to_all.11.rows_ref), custom_call_target="tpu_custom_call" | custom-call | flops 29360128 | bytes 1835008 | tf_op jit(solution)/shard_map/pallas_call | solution.py:134
  (3 shorter events, 0.0 us)
Async XLA Ops:
  3.0 40.7 %slice-start = ((s8[7340032]{0:T(1024)(128)(4,1)}), s8[4194304]{0:T(1024)(128)(4,1)S(1)}, s32[]{:S(2)}) async-start(s8[7340032]{0:T(1024)(128)(4,1)} %bitcast.5), calls=%async_computation.2 | async-start | bytes 8388608
  3.0 40.7 %slice-start.2 = ((s8[7340032]{0:T(1024)(128)(4,1)}), s8[4194304]{0:T(1024)(128)(4,1)S(1)}, s32[]{:S(2)}) async-start(s8[7340032]{0:T(1024)(128)(4,1)} %bitcast.8), calls=%async_computation.4 | async-start | bytes 8388608
  3.0 40.7 %slice-start.4 = ((s8[7340032]{0:T(1024)(128)(4,1)}), s8[4194304]{0:T(1024)(128)(4,1)S(1)}, s32[]{:S(2)}) async-start(s8[7340032]{0:T(1024)(128)(4,1)} %bitcast.11), calls=%async_computation.6 | async-start | bytes 8388608
  5.3 38.4 %slice-start.1 = ((s8[7340032]{0:T(1024)(128)(4,1)}), s8[3145728]{0:T(1024)(128)(4,1)S(1)}, s32[]{:S(2)}) async-start(s8[7340032]{0:T(1024)(128)(4,1)} %bitcast.5), calls=%async_computation.3 | async-start | bytes 6291456
  5.3 38.5 %slice-start.3 = ((s8[7340032]{0:T(1024)(128)(4,1)}), s8[3145728]{0:T(1024)(128)(4,1)S(1)}, s32[]{:S(2)}) async-start(s8[7340032]{0:T(1024)(128)(4,1)} %bitcast.8), calls=%async_computation.5 | async-start | bytes 6291456
  5.3 38.5 %slice-start.5 = ((s8[7340032]{0:T(1024)(128)(4,1)}), s8[3145728]{0:T(1024)(128)(4,1)S(1)}, s32[]{:S(2)}) async-start(s8[7340032]{0:T(1024)(128)(4,1)} %bitcast.11), calls=%async_computation.7 | async-start | bytes 6291456
  6.3 37.6 %copy-start = (s32[16,8]{0,1:T(8,128)S(1)}, s32[16,8]{0,1:T(8,128)}, u32[]{:S(2)}) copy-start(s32[16,8]{0,1:T(8,128)} %param.7) | copy-start | bytes 1540
  6.3 37.6 %copy-start.1 = (bf16[16,8]{0,1:T(8,128)(2,1)S(1)}, bf16[16,8]{0,1:T(8,128)(2,1)}, u32[]{:S(2)}) copy-start(bf16[16,8]{0,1:T(8,128)(2,1)} %param.8) | copy-start | bytes 772

commit v7 on v4

--- a/solution.py
+++ b/solution.py
@@ -10,10 +10,20 @@
 MIB = 1 << 20
 
 
+ORDER = ("x", "y", "z", "core")
+
+
 def routing(ids_t, rows):
     topk, tok_count = ids_t.shape
     row = lax.broadcasted_iota(jnp.int32, (rows, tok_count), 0)
-    expert = row >> 1
+    expert, rest = jnp.zeros_like(row), row >> 1
+    stride = {"x": 1, "y": lax.axis_size("x")}
+    stride["core"] = stride["y"] * lax.axis_size("y")
+    stride["z"] = stride["core"] * lax.axis_size("core")
+    for axis in reversed(ORDER):
+        size = lax.axis_size(axis)
+        expert = expert + (rest & (size - 1)) * stride[axis]
+        rest = rest >> (size.bit_length() - 1)
     used = jnp.zeros((rows, tok_count), jnp.float32)
     for k in range(topk):
         used = jnp.where(ids_t[k : k + 1, :] == expert, 1.0, used)
@@ -77,14 +87,14 @@
 
 
 def exchange(blocks):
-    return lax.all_to_all(blocks, ("node", "local"), split_axis=0, concat_axis=0, tiled=True)
+    return lax.all_to_all(blocks, ORDER, split_axis=0, concat_axis=0, tiled=True)
 
 
 def local(tokens, expert_ids, gate_values, w_gate, w_up, w_down):
     tok_count, width = tokens.shape
     topk = expert_ids.shape[1]
     hid = w_gate.shape[2]
-    experts = lax.axis_size("node") * lax.axis_size("local")
+    experts = lax.axis_size(ORDER)
     rows = experts * PAIR
     bf16 = jnp.bfloat16
     hbm = pl.BlockSpec(memory_space=pltpu.HBM)
@@ -134,17 +144,13 @@
 
 
 def solution(mesh):
+    axes = ("z", "core", "y", "x")
+    flat = P(axes, None)
+    whole = P(axes, None, None)
     return jax.shard_map(
         local,
-        mesh=mesh,
-        in_specs=(
-            P(("node", "local"), None),
-            P(("node", "local"), None),
-            P(("node", "local"), None),
-            P(("node", "local"), None, None),
-            P(("node", "local"), None, None),
-            P(("node", "local"), None, None),
-        ),
-        out_specs=P(("node", "local"), None),
+        mesh=jax.sharding.Mesh(mesh.devices.reshape(4, 2, 4, 4), axes),
+        in_specs=(flat, flat, flat, whole, whole, whole),
+        out_specs=flat,
         check_vma=False,
     )

time: 78.9 us -> 80.1 us (1.015)
  blocking collectives: 69.7 us -> 70.8 us
    all_to_all x2, blocking collectives: 69.7 us -> 70.8 us  [exchange(): lax.all_to_all(blocks, ORDER, split_axis=0, concat_axis=0, tiled=True)]
where the time goes in v7:
time: 80.1 us; the launch traced here: 80 us
  blocking collectives  70.8 us (88%)
  Pallas kernels  9.06 us (11%)
    all_to_all x2, blocking collectives, exchange(): lax.all_to_all(blocks, ORDER, split_axis=0, concat_axis=0, tiled=True)  70.8 us
    pallas_call x1, Pallas kernels, local(): pl.pallas_call(expert_kernel, out_shape=[jax.ShapeDtypeStruct((experts, P...  6.29 us
    pallas_call x1, Pallas kernels, local(): pl.pallas_call(dispatch_kernel, out_shape=jax.ShapeDtypeStruct((experts,...  1.73 us

profile of v7, /device:TPU:1, one launch (start us, length us, event | category | flops | bytes accessed | tf_op | source)
XLA Modules:
  0.0 80.0 jit_solution(8452315435663932856)
XLA Ops:
  0.0 0.0 slice-start
  0.0 0.0 slice-start.2
  0.0 0.0 slice-start.4
  0.0 0.0 slice-start.1
  0.0 0.0 slice-start.3
  0.0 0.0 slice-start.5
  0.0 1.7 %shard_map.64 = bf16[128,2,3584]{2,1,0:T(2,128)(2,1)S(1)} custom-call(s32[8,16]{1,0:T(8,128)} %bitcast.14, bf16[16,3584]{1,0:T(8,128)(2,1)} %tokens_hbm.1), custom_call_target="tpu_custom_call" | custom-call | flops 30000001024 | bytes 60000000 | tf_op jit(solution)/shard_map/pallas_call | solution.py:103
  1.8 0.0 copy-start
  1.8 0.0 copy-start.1
  1.8 39.0 %all_to_all.10.rows_ref = bf16[128,2,3584]{2,1,0:T(2,128)(2,1)S(1)} all-to-all(bf16[128,2,3584]{2,1,0:T(2,128)(2,1)S(1)} %shard_map.64), channel_id=1, replica_groups=mesh['z'=4,'core'=2,'y'=4,'x'=4] {'x','y','z','core'}, dimensions={0} | all-to-all | bytes 3670016 | tf_op jit(solution)/shard_map/all_to_all | solution.py:90
  40.8 0.0 slice-done
  40.8 0.0 slice-done.2
  40.8 0.0 slice-done.4
  40.8 0.0 slice-done.1
  40.8 0.0 slice-done.3
  40.8 0.0 slice-done.5
  40.8 0.0 copy-done
  40.9 0.0 copy-done.1
  40.9 6.3 %shard_map.65 = (bf16[128,2,3584]{2,1,0:T(2,128)(2,1)S(1)}, bf16[16,256]{1,0:T(8,128)(2,1)S(1)}) custom-call(bf16[128,2,3584]{2,1,0:T(2,128)(2,1)S(1)} %all_to_all.10.rows_ref, bf16[3584,1024]{1,0:T(8,128)(2,1)S(1)} %bitcast.7, bf16[3584,1024]{1,0:T(8,128)(2,1)S(1)} %bitcast.10, bf16[1024,3584]{1,0:T(8,128)(2,1)S(1)} %bitcast.13, s32[8,16]{1,0:T(8,128)S(1)} %bitcast.15, ...), custom_call_target="tpu_custom_call" | custom-call | flops 5637144576 | bytes 22020096 | tf_op jit(solution)/shard_map/pallas_call | solution.py:119
  47.2 31.8 %all_to_all.11.rows_ref = bf16[128,2,3584]{2,1,0:T(2,128)(2,1)S(1)} all-to-all(bf16[128,2,3584]{2,1,0:T(2,128)(2,1)S(1)} %get-tuple-element.8), channel_id=1, replica_groups=mesh['z'=4,'core'=2,'y'=4,'x'=4] {'x','y','z','core'}, dimensions={0} | all-to-all | bytes 3670016 | tf_op jit(solution)/shard_map/all_to_all | solution.py:90
  79.0 1.0 %shard_map.66 = bf16[16,3584]{1,0:T(8,128)(2,1)} custom-call(bf16[16,256]{1,0:T(8,128)(2,1)S(1)} %get-tuple-element.7.table_ref, bf16[128,2,3584]{2,1,0:T(2,128)(2,1)S(1)} %all_to_all.11.rows_ref), custom_call_target="tpu_custom_call" | custom-call | flops 29360128 | bytes 1835008 | tf_op jit(solution)/shard_map/pallas_call | solution.py:134
  (3 shorter events, 0.0 us)
Async XLA Ops:
  0.0 40.8 %slice-start = ((s8[7340032]{0:T(1024)(128)(4,1)}), s8[4194304]{0:T(1024)(128)(4,1)S(1)}, s32[]{:S(2)}) async-start(s8[7340032]{0:T(1024)(128)(4,1)} %bitcast.5), calls=%async_computation.2 | async-start | bytes 8388608
  0.0 40.8 %slice-start.2 = ((s8[7340032]{0:T(1024)(128)(4,1)}), s8[4194304]{0:T(1024)(128)(4,1)S(1)}, s32[]{:S(2)}) async-start(s8[7340032]{0:T(1024)(128)(4,1)} %bitcast.8), calls=%async_computation.4 | async-start | bytes 8388608
  0.0 40.8 %slice-start.4 = ((s8[7340032]{0:T(1024)(128)(4,1)}), s8[4194304]{0:T(1024)(128)(4,1)S(1)}, s32[]{:S(2)}) async-start(s8[7340032]{0:T(1024)(128)(4,1)} %bitcast.11), calls=%async_computation.6 | async-start | bytes 8388608
  0.0 40.8 %slice-start.1 = ((s8[7340032]{0:T(1024)(128)(4,1)}), s8[3145728]{0:T(1024)(128)(4,1)S(1)}, s32[]{:S(2)}) async-start(s8[7340032]{0:T(1024)(128)(4,1)} %bitcast.5), calls=%async_computation.3 | async-start | bytes 6291456
  0.0 40.8 %slice-start.3 = ((s8[7340032]{0:T(1024)(128)(4,1)}), s8[3145728]{0:T(1024)(128)(4,1)S(1)}, s32[]{:S(2)}) async-start(s8[7340032]{0:T(1024)(128)(4,1)} %bitcast.8), calls=%async_computation.5 | async-start | bytes 6291456
  0.0 40.8 %slice-start.5 = ((s8[7340032]{0:T(1024)(128)(4,1)}), s8[3145728]{0:T(1024)(128)(4,1)S(1)}, s32[]{:S(2)}) async-start(s8[7340032]{0:T(1024)(128)(4,1)} %bitcast.11), calls=%async_computation.7 | async-start | bytes 6291456
  1.8 39.1 %copy-start = (s32[16,8]{0,1:T(8,128)S(1)}, s32[16,8]{0,1:T(8,128)}, u32[]{:S(2)}) copy-start(s32[16,8]{0,1:T(8,128)} %param.7) | copy-start | bytes 1540
  1.8 39.1 %copy-start.1 = (bf16[16,8]{0,1:T(8,128)(2,1)S(1)}, bf16[16,8]{0,1:T(8,128)(2,1)}, u32[]{:S(2)}) copy-start(bf16[16,8]{0,1:T(8,128)(2,1)} %param.8) | copy-start | bytes 772

commit v8 on v4

--- a/solution.py
+++ b/solution.py
@@ -52,6 +52,7 @@
     experts, pair, width = rows_ref.shape
     rows = experts * pair
     hid = gate_ref.shape[1]
+    table_ref[...] = gate_table(ids_ref[...], gates_ref[...].astype(jnp.float32), rows)
     for n in range(width // TILE):
         columns = slice(n * TILE, (n + 1) * TILE)
         x_ref[:, columns] = rows_ref[:, :, columns].reshape(rows, TILE)
@@ -60,7 +61,6 @@
         gate = jnp.dot(x_ref[...], gate_ref[:, columns], preferred_element_type=jnp.float32)
         upper = jnp.dot(x_ref[...], up_ref[:, columns], preferred_element_type=jnp.float32)
         h_ref[:, columns] = (gate / (1.0 + jnp.exp(-gate)) * upper).astype(jnp.bfloat16)
-    table_ref[...] = gate_table(ids_ref[...], gates_ref[...].astype(jnp.float32), rows)
     for n in range(width // TILE):
         columns = slice(n * TILE, (n + 1) * TILE)
         block = jnp.dot(h_ref[...], down_ref[:, columns], preferred_element_type=jnp.float32)

time: 78.9 us -> 79 us (level)
  no operation moved by 1% of the time
where the time goes in v8:
time: 79 us; the launch traced here: 78.9 us
  blocking collectives  69.7 us (88%)
  Pallas kernels  9.04 us (11%)
    all_to_all x2, blocking collectives, exchange(): lax.all_to_all(blocks, ('node', 'local'), split_axis=0, concat_axis=0, ti...  69.7 us
    pallas_call x1, Pallas kernels, local(): pl.pallas_call(expert_kernel, out_shape=[jax.ShapeDtypeStruct((experts, P...  6.31 us
    pallas_call x1, Pallas kernels, local(): pl.pallas_call(dispatch_kernel, out_shape=jax.ShapeDtypeStruct((experts,...  1.7 us

profile of v8, /device:TPU:1, one launch (start us, length us, event | category | flops | bytes accessed | tf_op | source)
XLA Modules:
  0.0 78.9 jit_solution(7498224908965658381)
XLA Ops:
  0.0 0.0 slice-start
  0.0 0.0 slice-start.2
  0.0 0.0 slice-start.4
  0.0 0.0 slice-start.1
  0.0 0.0 slice-start.3
  0.0 0.0 slice-start.5
  0.0 1.7 %shard_map.64 = bf16[128,2,3584]{2,1,0:T(2,128)(2,1)S(1)} custom-call(s32[8,16]{1,0:T(8,128)} %bitcast.14, bf16[16,3584]{1,0:T(8,128)(2,1)} %tokens_hbm.1), custom_call_target="tpu_custom_call" | custom-call | flops 30000001024 | bytes 60000000 | tf_op jit(solution)/shard_map/pallas_call | solution.py:93
  1.7 0.0 copy-start
  1.8 0.0 copy-start.1
  1.8 38.2 %all_to_all.10.rows_ref = bf16[128,2,3584]{2,1,0:T(2,128)(2,1)S(1)} all-to-all(bf16[128,2,3584]{2,1,0:T(2,128)(2,1)S(1)} %shard_map.64), channel_id=1, replica_groups=mesh['node'=8,'local'=16] {'node','local'}, dimensions={0} | all-to-all | bytes 3670016 | tf_op jit(solution)/shard_map/all_to_all | solution.py:80
  40.0 0.0 slice-done
  40.0 0.0 slice-done.2
  40.0 0.0 slice-done.4
  40.0 0.0 slice-done.1
  40.0 0.0 slice-done.3
  40.0 0.0 slice-done.5
  40.0 0.0 copy-done
  40.0 0.0 copy-done.1
  40.1 6.3 %shard_map.65 = (bf16[128,2,3584]{2,1,0:T(2,128)(2,1)S(1)}, bf16[16,256]{1,0:T(8,128)(2,1)S(1)}) custom-call(bf16[128,2,3584]{2,1,0:T(2,128)(2,1)S(1)} %all_to_all.10.rows_ref, bf16[3584,1024]{1,0:T(8,128)(2,1)S(1)} %bitcast.7, bf16[3584,1024]{1,0:T(8,128)(2,1)S(1)} %bitcast.10, bf16[1024,3584]{1,0:T(8,128)(2,1)S(1)} %bitcast.13, s32[8,16]{1,0:T(8,128)S(1)} %bitcast.15, ...), custom_call_target="tpu_custom_call" | custom-call | flops 5637144576 | bytes 22020096 | tf_op jit(solution)/shard_map/pallas_call | solution.py:109
  46.4 31.5 %all_to_all.11.rows_ref = bf16[128,2,3584]{2,1,0:T(2,128)(2,1)S(1)} all-to-all(bf16[128,2,3584]{2,1,0:T(2,128)(2,1)S(1)} %get-tuple-element.8), channel_id=1, replica_groups=mesh['node'=8,'local'=16] {'node','local'}, dimensions={0} | all-to-all | bytes 3670016 | tf_op jit(solution)/shard_map/all_to_all | solution.py:80
  77.9 1.0 %shard_map.66 = bf16[16,3584]{1,0:T(8,128)(2,1)} custom-call(bf16[16,256]{1,0:T(8,128)(2,1)S(1)} %get-tuple-element.7.table_ref, bf16[128,2,3584]{2,1,0:T(2,128)(2,1)S(1)} %all_to_all.11.rows_ref), custom_call_target="tpu_custom_call" | custom-call | flops 29360128 | bytes 1835008 | tf_op jit(solution)/shard_map/pallas_call | solution.py:124
  (3 shorter events, 0.0 us)
Async XLA Ops:
  0.0 40.0 %slice-start = ((s8[7340032]{0:T(1024)(128)(4,1)}), s8[4194304]{0:T(1024)(128)(4,1)S(1)}, s32[]{:S(2)}) async-start(s8[7340032]{0:T(1024)(128)(4,1)} %bitcast.5), calls=%async_computation.2 | async-start | bytes 8388608
  0.0 40.0 %slice-start.2 = ((s8[7340032]{0:T(1024)(128)(4,1)}), s8[4194304]{0:T(1024)(128)(4,1)S(1)}, s32[]{:S(2)}) async-start(s8[7340032]{0:T(1024)(128)(4,1)} %bitcast.8), calls=%async_computation.4 | async-start | bytes 8388608
  0.0 40.0 %slice-start.4 = ((s8[7340032]{0:T(1024)(128)(4,1)}), s8[4194304]{0:T(1024)(128)(4,1)S(1)}, s32[]{:S(2)}) async-start(s8[7340032]{0:T(1024)(128)(4,1)} %bitcast.11), calls=%async_computation.6 | async-start | bytes 8388608
  0.0 40.0 %slice-start.1 = ((s8[7340032]{0:T(1024)(128)(4,1)}), s8[3145728]{0:T(1024)(128)(4,1)S(1)}, s32[]{:S(2)}) async-start(s8[7340032]{0:T(1024)(128)(4,1)} %bitcast.5), calls=%async_computation.3 | async-start | bytes 6291456
  0.0 40.0 %slice-start.3 = ((s8[7340032]{0:T(1024)(128)(4,1)}), s8[3145728]{0:T(1024)(128)(4,1)S(1)}, s32[]{:S(2)}) async-start(s8[7340032]{0:T(1024)(128)(4,1)} %bitcast.8), calls=%async_computation.5 | async-start | bytes 6291456
  0.0 40.0 %slice-start.5 = ((s8[7340032]{0:T(1024)(128)(4,1)}), s8[3145728]{0:T(1024)(128)(4,1)S(1)}, s32[]{:S(2)}) async-start(s8[7340032]{0:T(1024)(128)(4,1)} %bitcast.11), calls=%async_computation.7 | async-start | bytes 6291456
  1.7 38.3 %copy-start = (s32[16,8]{0,1:T(8,128)S(1)}, s32[16,8]{0,1:T(8,128)}, u32[]{:S(2)}) copy-start(s32[16,8]{0,1:T(8,128)} %param.7) | copy-start | bytes 1540
  1.8 38.3 %copy-start.1 = (bf16[16,8]{0,1:T(8,128)(2,1)S(1)}, bf16[16,8]{0,1:T(8,128)(2,1)}, u32[]{:S(2)}) copy-start(bf16[16,8]{0,1:T(8,128)(2,1)} %param.8) | copy-start | bytes 772
